TPU v7x, 32 devices: a whole 2x2x4 slice. The times are simulated.
32 devices in a mesh: dp: 8 (over y, x, core), tensor: 4 (over z).
Axes of the slice: x: 2, y: 2, z: 4, core: 2. Of those that a mesh axis runs over, the one named last changes fastest.
Arguments:
- tokens: bfloat16 [24576, 1024], P(('dp', 'tensor')), may hold values from -6 to 6
- positions: int32 [24576], P('dp'), may hold values from 0 to 4092, as said below
- first_gain: bfloat16 [1024], replicated, may hold values from 0.099609375 to 1.8984375
- w_query: bfloat16 [1024, 2048], P(None, 'tensor'), may hold values from -0.1875 to 0.1875
- key_matrix: bfloat16 [1024, 1024], P(None, 'tensor'), may hold values from -0.1875 to 0.1875
- value_matrix: bfloat16 [1024, 1024], P(None, 'tensor'), may hold values from -0.1875 to 0.1875
- query_gain: bfloat16 [128], replicated, may hold values from 0.099609375 to 1.8984375
- key_gain: bfloat16 [128], replicated, may hold values from 0.099609375 to 1.8984375
- w_output: bfloat16 [2048, 1024], P('tensor'), may hold values from -0.5 to 0.5
- second_gain: bfloat16 [1024], replicated, may hold values from 0.099609375 to 1.8984375
- w_gate: bfloat16 [1024, 3072], P(None, 'tensor'), may hold values from -0.1875 to 0.1875
- w_up: bfloat16 [1024, 3072], P(None, 'tensor'), may hold values from -0.1875 to 0.1875
- w_down: bfloat16 [3072, 1024], P('tensor'), may hold values from -0.109375 to 0.109375
- out_grad: bfloat16 [24576, 1024], P(('dp', 'tensor')), may hold values from -6 to 6
Outputs:
- layer_out: bfloat16 [24576, 1024], P(('dp', 'tensor'))
- input_grad: bfloat16 [24576, 1024], P(('dp', 'tensor'))
- first_gain_grad: float32 [1024], P('tensor')
- query_weight_grad: float32 [1024, 2048], P(None, 'tensor')
- key_weight_grad: float32 [1024, 1024], P(None, 'tensor')
- value_weight_grad: float32 [1024, 1024], P(None, 'tensor')
- query_gain_grad: float32 [128], P('tensor')
- key_gain_grad: float32 [128], P('tensor')
- output_weight_grad: float32 [2048, 1024], P('tensor')
- second_gain_grad: float32 [1024], P('tensor')
- gate_weight_grad: float32 [1024, 3072], P(None, 'tensor')
- up_weight_grad: float32 [1024, 3072], P(None, 'tensor')
- down_weight_grad: float32 [3072, 1024], P('tensor')
Inputs may be any that keep to these rules, and one draw needn't show every extreme that they name: Within each aligned block of 1024 rows (one sequence) positions start at 0 and rise by 1 to 4 from one row to the next.
All inputs are finite; a program needn't handle non-finite values.
Results may differ from a plain program's by a relative error of at most 0.023.
Values may be sent and summed in bfloat16 or wider, within the bound.
A program may use at most 256 MiB of HBM per device.

v0:
```python
import math

import jax
import jax.numpy as jnp
from jax import lax
from jax.sharding import PartitionSpec as P

SEQUENCE_TOKENS = 1024


epsilon = 1e-06
rope_base = 1000000.0


def norm_forward(value, gain):
    inverse = lax.rsqrt(jnp.mean(value * value, axis=-1, keepdims=True) + epsilon)
    unit = value * inverse
    return (unit * gain, unit, inverse)


def norm_backward(grad, unit, inverse, gain):
    scaled = grad * gain
    back = inverse * (scaled - unit * jnp.mean(scaled * unit, axis=-1, keepdims=True))
    share = jnp.sum((grad * unit).reshape(-1, grad.shape[-1]), axis=0)
    return (back, share)


def rotate(value, cosine, sine):
    half = value.shape[-1] // 2
    first = value[..., :half]
    second = value[..., half:]
    return jnp.concatenate(
        [first * cosine - second * sine, second * cosine + first * sine], axis=-1
    )


def unrotate(grad, cosine, sine):
    half = grad.shape[-1] // 2
    first = grad[..., :half]
    second = grad[..., half:]
    return jnp.concatenate(
        [first * cosine + second * sine, second * cosine - first * sine], axis=-1
    )


def times_plain(left, right):
    return jnp.dot(left, right, preferred_element_type=jnp.float32)


def times_left(left, right):
    return lax.dot_general(
        left, right, (((0,), (0,)), ((), ())), preferred_element_type=jnp.float32
    )


def times_right(left, right):
    return lax.dot_general(
        left, right, (((1,), (1,)), ((), ())), preferred_element_type=jnp.float32
    )


def causal(start, count, key_rows):
    row_ids = start + lax.broadcasted_iota(jnp.int32, (count, key_rows), 0)
    col_ids = lax.broadcasted_iota(jnp.int32, (count, key_rows), 1)
    return col_ids <= row_ids


def on_device(
    tokens,
    positions,
    first_gain,
    w_query,
    key_matrix,
    value_matrix,
    query_gain,
    key_gain,
    w_output,
    second_gain,
    w_gate,
    w_up,
    w_down,
    out_grad,
):
    rows = tokens.shape[0]
    width = query_gain.shape[0]
    total = positions.shape[0]
    seqs = total // SEQUENCE_TOKENS
    q_heads = w_query.shape[1] // width
    kv_heads = key_matrix.shape[1] // width
    group = q_heads // kv_heads
    block = min(512, SEQUENCE_TOKENS)
    blocks = SEQUENCE_TOKENS // block
    scale = width ** (-0.5)
    gain_one = first_gain.astype(jnp.float32)
    gain_two = second_gain.astype(jnp.float32)
    gain_q = query_gain.astype(jnp.float32)
    gain_k = key_gain.astype(jnp.float32)
    rate = jnp.exp(-math.log(rope_base) * 2.0 * jnp.arange(width // 2, dtype=jnp.float32) / width)
    angles = positions.astype(jnp.float32)[:, None] * rate[None, :]
    cosine = jnp.cos(angles)[:, None, :]
    sine = jnp.sin(angles)[:, None, :]
    resid = tokens.astype(jnp.float32)
    normed_one, unit_one, inv_one = norm_forward(resid, gain_one)
    first_rows = lax.all_gather(normed_one.astype(jnp.bfloat16), "tensor", axis=0, tiled=True)
    q_raw = times_plain(first_rows, w_query).reshape(total, q_heads, width)
    key_unnormed = times_plain(first_rows, key_matrix).reshape(total, kv_heads, width)
    v_low = times_plain(first_rows, value_matrix).astype(jnp.bfloat16)
    q_normed, unit_q, inv_q = norm_forward(q_raw, gain_q)
    k_normed, unit_k, inv_k = norm_forward(key_unnormed, gain_k)
    q_five = (
        rotate(q_normed, cosine, sine)
        .astype(jnp.bfloat16)
        .reshape(seqs, SEQUENCE_TOKENS, kv_heads, group, width)
    )
    k_four = (
        rotate(k_normed, cosine, sine)
        .astype(jnp.bfloat16)
        .reshape(seqs, SEQUENCE_TOKENS, kv_heads, width)
    )
    v_four = v_low.reshape(seqs, SEQUENCE_TOKENS, kv_heads, width)

    def seq_forward(item):
        q_seq, k_seq, v_seq = item
        outputs = []
        sums = []
        for blk in range(blocks):
            finish = (blk + 1) * block
            q_blk = q_seq[blk * block : finish]
            scores = (
                jnp.einsum(
                    "qkgd,ckd->kgqc", q_blk, k_seq[:finish], preferred_element_type=jnp.float32
                )
                * scale
            )
            scores = jnp.where(causal(blk * block, block, finish)[None, None], scores, -1e30)
            top = jnp.max(scores, axis=-1, keepdims=True)
            expo = jnp.exp(scores - top)
            totals = jnp.sum(expo, axis=-1, keepdims=True)
            probs = (expo / totals).astype(jnp.bfloat16)
            outputs.append(
                jnp.einsum(
                    "kgqc,ckd->qkgd", probs, v_seq[:finish], preferred_element_type=jnp.float32
                ).astype(jnp.bfloat16)
            )
            sums.append(top + jnp.log(totals))
        return (jnp.concatenate(outputs, axis=0), jnp.concatenate(sums, axis=2))

    heads_five, log_sums = lax.map(seq_forward, (q_five, k_four, v_four))
    heads = heads_five.reshape(total, q_heads * width)
    mid = resid + lax.psum_scatter(
        times_plain(lax.slice_in_dim(heads, 0, lax.axis_size("tensor") * rows, axis=0), w_output),
        "tensor",
        scatter_dimension=0,
        tiled=True,
    )
    normed_two, unit_two, inv_two = norm_forward(mid, gain_two)
    second_rows = lax.all_gather(normed_two.astype(jnp.bfloat16), "tensor", axis=0, tiled=True)
    gate = times_plain(second_rows, w_gate)
    up_part = times_plain(second_rows, w_up)
    sigma = jax.nn.sigmoid(gate)
    hidden = (gate * sigma * up_part).astype(jnp.bfloat16)
    layer_out = (
        mid
        + lax.psum_scatter(
            times_plain(
                lax.slice_in_dim(hidden, 0, lax.axis_size("tensor") * rows, axis=0), w_down
            ).astype(jnp.bfloat16),
            "tensor",
            scatter_dimension=0,
            tiled=True,
        ).astype(jnp.float32)
    ).astype(jnp.bfloat16)
    grad_out = out_grad.astype(jnp.float32)
    grad_rows = lax.all_gather(out_grad, "tensor", axis=0, tiled=True)
    down_wgrad = times_left(hidden, grad_rows)
    hidden_grad = times_right(grad_rows, w_down)
    gate_low = (hidden_grad * up_part * sigma * (1.0 + gate * (1.0 - sigma))).astype(jnp.bfloat16)
    up_low = (hidden_grad * gate * sigma).astype(jnp.bfloat16)
    gate_wgrad = times_left(second_rows, gate_low)
    up_wgrad = times_left(second_rows, up_low)
    gate_piece = lax.slice_in_dim(gate_low, 0, lax.axis_size("tensor") * rows, axis=0)
    up_piece = lax.slice_in_dim(up_low, 0, lax.axis_size("tensor") * rows, axis=0)
    normed_grad_two = lax.psum_scatter(
        (times_right(gate_piece, w_gate) + times_right(up_piece, w_up)).astype(jnp.bfloat16),
        "tensor",
        scatter_dimension=0,
        tiled=True,
    ).astype(jnp.float32)
    back_two, share_two = norm_backward(normed_grad_two, unit_two, inv_two, gain_two)
    mid_grad = grad_out + back_two
    branch_rows = lax.all_gather(mid_grad.astype(jnp.bfloat16), "tensor", axis=0, tiled=True)
    out_wgrad = times_left(heads, branch_rows)
    heads_grad = times_right(branch_rows, w_output).astype(jnp.bfloat16)
    grad_five = heads_grad.reshape(seqs, SEQUENCE_TOKENS, kv_heads, group, width)

    def seq_backward(item):
        q_seq, k_seq, v_seq, d_seq, lse_seq = item
        query_parts = []
        key_grad = jnp.zeros((SEQUENCE_TOKENS, kv_heads, width), jnp.float32)
        value_grad = jnp.zeros((SEQUENCE_TOKENS, kv_heads, width), jnp.float32)
        for blk in range(blocks):
            finish = (blk + 1) * block
            q_blk = q_seq[blk * block : finish]
            d_blk = d_seq[blk * block : finish]
            key_rows = k_seq[:finish]
            value_rows = v_seq[:finish]
            scores = (
                jnp.einsum("qkgd,ckd->kgqc", q_blk, key_rows, preferred_element_type=jnp.float32)
                * scale
            )
            lse_blk = lse_seq[:, :, blk * block : finish]
            probs = jnp.where(
                causal(blk * block, block, finish)[None, None], jnp.exp(scores - lse_blk), 0.0
            )
            dprobs = jnp.einsum(
                "qkgd,ckd->kgqc", d_blk, value_rows, preferred_element_type=jnp.float32
            )
            delta = jnp.sum(probs * dprobs, axis=-1, keepdims=True)
            dscore = (probs * (dprobs - delta)).astype(jnp.bfloat16)
            value_grad = value_grad.at[:finish].add(
                jnp.einsum(
                    "kgqc,qkgd->ckd",
                    probs.astype(jnp.bfloat16),
                    d_blk,
                    preferred_element_type=jnp.float32,
                )
            )
            key_grad = key_grad.at[:finish].add(
                jnp.einsum("kgqc,qkgd->ckd", dscore, q_blk, preferred_element_type=jnp.float32)
                * scale
            )
            query_parts.append(
                jnp.einsum("kgqc,ckd->qkgd", dscore, key_rows, preferred_element_type=jnp.float32)
                * scale
            )
        return (jnp.concatenate(query_parts, axis=0), key_grad, value_grad)

    dq_five, dk_four, dv_four = lax.map(seq_backward, (q_five, k_four, v_four, grad_five, log_sums))
    dq_back, share_q = norm_backward(
        unrotate(dq_five.reshape(total, q_heads, width), cosine, sine), unit_q, inv_q, gain_q
    )
    dk_back, share_k = norm_backward(
        unrotate(dk_four.reshape(total, kv_heads, width), cosine, sine), unit_k, inv_k, gain_k
    )
    dq_low = dq_back.reshape(total, q_heads * width).astype(jnp.bfloat16)
    dk_low = dk_back.reshape(total, kv_heads * width).astype(jnp.bfloat16)
    dv_low = dv_four.reshape(total, kv_heads * width).astype(jnp.bfloat16)
    query_wgrad = times_left(first_rows, dq_low)
    key_wgrad = times_left(first_rows, dk_low)
    value_wgrad = times_left(first_rows, dv_low)
    term = times_right(dq_low, w_query)
    term = term + times_right(dk_low, key_matrix)
    normed_grad_one = lax.psum_scatter(
        (term + times_right(dv_low, value_matrix)).astype(jnp.bfloat16),
        "tensor",
        scatter_dimension=0,
        tiled=True,
    ).astype(jnp.float32)
    back_one, share_one = norm_backward(normed_grad_one, unit_one, inv_one, gain_one)
    input_grad = (mid_grad + back_one).astype(jnp.bfloat16)
    part_one, part_two, part_q, part_k = (
        lax.psum_scatter(share_one, "tensor", scatter_dimension=0, tiled=True),
        lax.psum_scatter(share_two, "tensor", scatter_dimension=0, tiled=True),
        lax.psum_scatter(share_q, "tensor", scatter_dimension=0, tiled=True),
        lax.psum_scatter(share_k, "tensor", scatter_dimension=0, tiled=True),
    )
    (
        query_wgrad,
        key_wgrad,
        value_wgrad,
        out_wgrad,
        gate_wgrad,
        up_wgrad,
        down_wgrad,
        part_one,
        part_two,
        part_q,
        part_k,
    ) = (
        lax.psum(query_wgrad.astype(jnp.bfloat16), "dp").astype(jnp.float32),
        lax.psum(key_wgrad.astype(jnp.bfloat16), "dp").astype(jnp.float32),
        lax.psum(value_wgrad.astype(jnp.bfloat16), "dp").astype(jnp.float32),
        lax.psum(out_wgrad.astype(jnp.bfloat16), "dp").astype(jnp.float32),
        lax.psum(gate_wgrad.astype(jnp.bfloat16), "dp").astype(jnp.float32),
        lax.psum(up_wgrad.astype(jnp.bfloat16), "dp").astype(jnp.float32),
        lax.psum(down_wgrad.astype(jnp.bfloat16), "dp").astype(jnp.float32),
        lax.psum(part_one.astype(jnp.bfloat16), "dp").astype(jnp.float32),
        lax.psum(part_two.astype(jnp.bfloat16), "dp").astype(jnp.float32),
        lax.psum(part_q.astype(jnp.bfloat16), "dp").astype(jnp.float32),
        lax.psum(part_k.astype(jnp.bfloat16), "dp").astype(jnp.float32),
    )
    return (
        layer_out,
        input_grad,
        part_one,
        query_wgrad,
        key_wgrad,
        value_wgrad,
        part_q,
        part_k,
        out_wgrad,
        part_two,
        gate_wgrad,
        up_wgrad,
        down_wgrad,
    )


def solution(mesh):
    placed = (
        P(("dp", "tensor"), None),
        P("dp"),
        P(),
        P(None, "tensor"),
        P(None, "tensor"),
        P(None, "tensor"),
        P(),
        P(),
        P("tensor", None),
        P(),
        P(None, "tensor"),
        P(None, "tensor"),
        P("tensor", None),
        P(("dp", "tensor"), None),
    )
    return jax.shard_map(
        on_device,
        mesh=mesh,
        in_specs=placed,
        out_specs=(
            P(("dp", "tensor"), None),
            P(("dp", "tensor"), None),
            P("tensor"),
            P(None, "tensor"),
            P(None, "tensor"),
            P(None, "tensor"),
            P("tensor"),
            P("tensor"),
            P("tensor", None),
            P("tensor"),
            P(None, "tensor"),
            P(None, "tensor"),
            P("tensor", None),
        ),
        check_vma=False,
    )
```

profile of v0, /device:TPU:0, one launch (start us, length us, event | category | flops | bytes accessed | tf_op | source)
XLA Modules:
  0.0 1634.3 jit_solution(14917311365436173098)
XLA Ops:
  20.6 111.1 %all-gather.5.cloned.1.call-done = bf16[3072,1024]{1,0:T(8,128)(2,1)} async-done(((bf16[768,1024]{1,0:T(8,128)(2,1)}), bf16[3072,1024]{1,0:T(8,128)(2,1)}) %all-gather.5.cloned.1.call-update) | async-done | bytes 6291472 | tf_op jit(solution)/shard_map/all_gather | solution.py:104
  131.7 9.3 multiply_reduce_fusion.1
  174.5 7.4 copy.111
  188.3 16.9 %copy.103 = f32[3072,2,128]{2,0,1:T(8,128)} copy(f32[3072,2,128]{0,2,1:T(8,128)} %bitcast.478) | data formatting | bytes 6291456 | tf_op jit(solution)/shard_map/reshape | solution.py:106
  231.6 84.9 %while.35 = (s32[]{:T(128)}, bf16[3,1024,2,2,128]{4,3,2,1,0:T(2,128)(2,1)}, f32[3,2,2,1024,1]{3,2,1,4,0:T(2,128)S(1)}, bf16[3,1024,2,128]{3,2,1,0:T(2,128)(2,1)}...) while((s32[]{:T(128)}, ...), condition=%wide.region_8.9_spmd, body=%wide.region_3.8_spmd.sunk | while | flops 1651769856 | bytes 103455408 | solution.py:148
  322.2 8.2 fusion.118
  331.1 209.6 %reduce-scatter.5.cloned.1.call-done = f32[768,1024]{1,0:T(8,128)} async-done(((f32[3072,1024]{1,0:T(8,128)}), f32[768,1024]{1,0:T(8,128)}) %reduce-scatter.5.cloned.1.call-update) | async-done | bytes 3145744 | tf_op jit(solution)/shard_map/reduce_scatter | solution.py:150
  546.8 115.9 %all-gather.7.cloned.1.call-done = bf16[3072,1024]{1,0:T(8,128)(2,1)} async-done(((bf16[768,1024]{1,0:T(8,128)(2,1)}), bf16[3072,1024]{1,0:T(8,128)(2,1)}) %all-gather.7.cloned.1.call-update) | async-done | bytes 6291472 | tf_op jit(solution)/shard_map/all_gather | solution.py:157
  662.8 10.6 fusion.119
  673.4 7.3 fusion.120
  680.7 97.1 %all-gather.9.cloned.1.call-done = bf16[3072,1024]{1,0:T(8,128)(2,1)} async-done(((bf16[768,1024]{1,0:T(8,128)(2,1)}), bf16[3072,1024]{1,0:T(8,128)(2,1)}) %all-gather.9.cloned.1.call-update) | async-done | bytes 6291472 | tf_op jit(solution)/shard_map/all_gather | solution.py:174
  777.8 18.9 %multiply_convert_fusion = (bf16[3072,768]{1,0:T(8,128)(2,1)}, bf16[3072,768]{1,0:T(8,128)(2,1)}, bf16[3072,768]{1,0:T(8,128)(2,1)}) fusion(f32[3072,768]{1,0:T(8,128)} %fusion.119, f32[3072,768]{1,0:T(8,128)} %fusion.120, bf16[3072,1024]{1,0:T(8,128)(2,1)} %all-gather.9.cloned.1.call-done, bf16[768,1024]{1,0:T(8,128)(2,1)S(1)} %copy-done), kind=kOutput, calls=%fused_computation.122 | convolution fusion | flops 4869586944 | bytes 40894464 | tf_op jit(solution)/shard_map/dot_general | solution.py:57
  804.0 7.5 add_convert_fusion.1
  811.7 108.9 %reduce-scatter.9.cloned.1.call-done = bf16[768,1024]{1,0:T(8,128)(2,1)} async-done(((bf16[3072,1024]{1,0:T(8,128)(2,1)}), bf16[768,1024]{1,0:T(8,128)(2,1)}) %reduce-scatter.9.cloned.1.call-update) | async-done | bytes 1572880 | tf_op jit(solution)/shard_map/reduce_scatter | solution.py:183
  929.6 9.7 convolution_convert_fusion.3
  939.3 8.5 convolution_convert_fusion.4
  954.2 90.2 %all-gather.11.cloned.1.call-done = bf16[3072,1024]{1,0:T(8,128)(2,1)} async-done(((bf16[768,1024]{1,0:T(8,128)(2,1)}), bf16[3072,1024]{1,0:T(8,128)(2,1)}) %all-gather.11.cloned.1.call-update) | async-done | bytes 6291472 | tf_op jit(solution)/shard_map/all_gather | solution.py:191
  1044.4 7.7 convolution_convert_fusion.1
  1057.6 144.3 %while.36 = (s32[]{:T(128)}, f32[3,1024,2,2,128]{4,1,0,3,2:T(8,128)}, f32[3,1024,2,128]{3,1,0,2:T(8,128)}, bf16[3,1024,2,128]{1,3,2,0:T(8,128)(2,1)}, bf16[3,102...) while((s32[]{:T(128)}, ...), condition=%wide.region_17.18_spmd, body=%wide.region_14.17_spmd.sunk | while | flops 4076466688 | bytes 261514224 | solution.py:238
  1248.6 8.4 convolution_convert_fusion.6
  1262.6 7.4 convolution_convert_fusion.7
  1273.2 8.5 fusion.123
  1288.4 12.7 add_convert_fusion
  1301.2 9.4 convolution_convert_fusion
  1345.2 11.8 copy.129
  1357.0 8.6 copy.124
  1365.6 13.4 copy.125
  1386.4 7.9 all-reduce.11.cloned.1.call-done
  1407.1 100.5 %reduce-scatter.11.cloned.1.call-done = bf16[768,1024]{1,0:T(8,128)(2,1)} async-done(((bf16[3072,1024]{1,0:T(8,128)(2,1)}), bf16[768,1024]{1,0:T(8,128)(2,1)}) %reduce-scatter.11.cloned.1.call-update) | async-done | bytes 1572880 | tf_op jit(solution)/shard_map/reduce_scatter | solution.py:253
  1510.2 18.4 %all-reduce.6 = (bf16[1024]{0:T(1024)(128)(2,1)S(1)}, bf16[128]{0:T(256)(128)(2,1)S(1)}, bf16[128]{0:T(256)(128)(2,1)S(1)}, bf16[1024]{0:T(1024)(128)(2,1)S(1)}) all-reduce(f32[1024]{0:T(1024)S(1)} %get-tuple-element.314, f32[128]{0:T(128)S(1)} %fusion.86, f32[128]{0:T(128)S(1)} %fusion.108, ...), channel_id=6, replica_groups=mesh['dp'=8,'tensor'=4] {'tensor'}, use_global_device_ids=true, to_apply=%region_23.24.clone | all-reduce | flops 2304 | bytes 13824
  1528.9 12.6 all-reduce.7
  1543.6 78.0 %reduce-scatter.7.cloned.1.call-done = bf16[768,1024]{1,0:T(8,128)(2,1)} async-done(((bf16[3072,1024]{1,0:T(8,128)(2,1)}), bf16[768,1024]{1,0:T(8,128)(2,1)}) %reduce-scatter.7.cloned.1.call-update) | async-done | bytes 1572880 | tf_op jit(solution)/shard_map/reduce_scatter | solution.py:164
  (478 shorter events, 474.1 us)
Async XLA Ops:
  7.2 770.6 %copy-start = (bf16[768,1024]{1,0:T(8,128)(2,1)S(1)}, bf16[768,1024]{1,0:T(8,128)(2,1)}, u32[]{:S(2)}) copy-start(bf16[768,1024]{1,0:T(8,128)(2,1)} %param.42) | copy-start | bytes 4718596
  7.2 124.4 %all-gather.5.cloned.1.call-start = ((), (), s32[]{:S(2)}) async-start(), calls=%async_computation.4 | async-start | bytes 7864320 | tf_op jit(solution)/shard_map/all_gather | solution.py:104
  13.5 527.3 %reduce-scatter.5.cloned.1.call-start = ((), (), s32[]{:S(2)}) async-start(), calls=%async_computation.5 | async-start | bytes 15728640 | tf_op jit(solution)/shard_map/reduce_scatter | solution.py:150
  13.6 134.0 %copy-start.62 = (f32[128]{0:T(128)}, f32[128]{0:T(128)S(1)}, u32[]{:S(2)}) copy-start(f32[128]{0:T(128)S(1)} %convert_element_type.203) | copy-start | bytes 1540
  13.6 191.6 %copy-start.65 = (f32[128]{0:T(128)}, f32[128]{0:T(128)S(1)}, u32[]{:S(2)}) copy-start(f32[128]{0:T(128)S(1)} %convert_element_type.201) | copy-start | bytes 1540
  20.6 187.2 %copy-start.20 = (f32[3072,64]{1,0:T(8,128)}, f32[3072,64]{1,0:T(8,128)S(1)}, u32[]{:S(2)}) copy-start(f32[3072,64]{1,0:T(8,128)S(1)} %get-tuple-element.394) | copy-start | bytes 2359300
  330.5 210.3 %copy-start.18 = (bf16[768,1024]{1,0:T(8,128)(2,1)S(1)}, bf16[768,1024]{1,0:T(8,128)(2,1)}, u32[]{:S(2)}) copy-start(bf16[768,1024]{1,0:T(8,128)(2,1)} %param.30) | copy-start | bytes 4718596
  330.5 332.3 %all-gather.7.cloned.1.call-start = ((), (), s32[]{:S(2)}) async-start(), calls=%async_computation.6 | async-start | bytes 7864320 | tf_op jit(solution)/shard_map/all_gather | solution.py:157
  331.1 593.6 %copy-start.49 = (f32[1024]{0:T(1024)}, f32[1024]{0:T(1024)S(1)}, u32[]{:S(2)}) copy-start(f32[1024]{0:T(1024)S(1)} %convert_element_type.204) | copy-start | bytes 12292
  543.1 381.7 %copy-start.51 = (f32[768]{0:T(1024)}, f32[768]{0:T(1024)S(1)}, u32[]{:S(2)}) copy-start(f32[768]{0:T(1024)S(1)} %add_rsqrt_fusion.2) | copy-start | bytes 9220
  544.7 118.1 %copy-start.71 = (bf16[1024,768]{1,0:T(8,128)(2,1)S(1)}, bf16[1024,768]{1,0:T(8,128)(2,1)}, u32[]{:S(2)}) copy-start(bf16[1024,768]{1,0:T(8,128)(2,1)} %param.40) | copy-start | bytes 4718596
  546.2 231.6 %all-gather.9.cloned.1.call-start = ((), (), s32[]{:S(2)}) async-start(), calls=%async_computation.8 | async-start | bytes 7864320 | tf_op jit(solution)/shard_map/all_gather | solution.py:174
  546.8 373.9 %reduce-scatter.9.cloned.1.call-start = ((), (), s32[]{:S(2)}) async-start(), calls=%async_computation.9 | async-start | bytes 7864320 | tf_op jit(solution)/shard_map/reduce_scatter | solution.py:183
  811.5 113.3 %copy-start.29 = (bf16[768,1024]{1,0:T(8,128)(2,1)S(1)}, bf16[768,1024]{1,0:T(8,128)(2,1)}, u32[]{:S(2)}) copy-start(bf16[768,1024]{1,0:T(8,128)(2,1)} %param.43) | copy-start | bytes 4718596
  811.5 232.9 %all-gather.11.cloned.1.call-start = ((), (), s32[]{:S(2)}) async-start(), calls=%async_computation.10 | async-start | bytes 7864320 | tf_op jit(solution)/shard_map/all_gather | solution.py:191
  928.3 465.9 %all-reduce.11.cloned.1.call-start = ((), (), s32[]{:S(2)}) async-start(), calls=%async_computation.12 | async-start | bytes 15728640 | tf_op jit(solution)/shard_map/psum | solution.py:280
  929.6 18.2 %slice-start.8 = ((s8[6291456]{0:T(1024)(128)(4,1)}), s8[4194304]{0:T(1024)(128)(4,1)S(1)}, s32[]{:S(2)}) async-start(s8[6291456]{0:T(1024)(128)(4,1)} %bitcast.495), calls=%async_computation.21 | async-start | bytes 8388608
  929.6 18.2 %slice-start.10 = ((s8[4718592]{0:T(1024)(128)(4,1)}), s8[4194304]{0:T(1024)(128)(4,1)S(1)}, s32[]{:S(2)}) async-start(s8[4718592]{0:T(1024)(128)(4,1)} %bitcast.497), calls=%async_computation.23 | async-start | bytes 8388608
  947.9 96.5 %copy-start.75 = (bf16[512,1024]{1,0:T(8,128)(2,1)S(1)}, bf16[512,1024]{1,0:T(8,128)(2,1)}, u32[]{:S(2)}) copy-start(bf16[512,1024]{1,0:T(8,128)(2,1)} %param.38) | copy-start | bytes 3145732
  1248.6 14.0 copy-start.36
  1273.1 234.5 %reduce-scatter.11.cloned.1.call-start = ((), (), s32[]{:S(2)}) async-start(), calls=%async_computation.11 | async-start | bytes 7864320 | tf_op jit(solution)/shard_map/reduce_scatter | solution.py:253
  1301.1 320.6 %reduce-scatter.7.cloned.1.call-start = ((), (), s32[]{:S(2)}) async-start(), calls=%async_computation.7 | async-start | bytes 7864320 | tf_op jit(solution)/shard_map/reduce_scatter | solution.py:164
  1345.2 20.4 %slice-start.2 = ((s8[6291456]{0:T(1024)(128)(4,1)}), s8[4194304]{0:T(1024)(128)(4,1)S(1)}, s32[]{:S(2)}) async-start(s8[6291456]{0:T(1024)(128)(4,1)} %bitcast.476), calls=%async_computation.15 | async-start | bytes 8388608
  1357.0 23.9 %slice-start.4 = ((s8[6291456]{0:T(1024)(128)(4,1)}), s8[4194304]{0:T(1024)(128)(4,1)S(1)}, s32[]{:S(2)}) async-start(s8[6291456]{0:T(1024)(128)(4,1)} %bitcast.480), calls=%async_computation.17 | async-start | bytes 8388608
  1365.6 15.2 slice-start.5
  1403.4 104.2 %copy-start.19 = (bf16[768,1024]{1,0:T(8,128)(2,1)S(1)}, bf16[768,1024]{1,0:T(8,128)(2,1)}, u32[]{:S(2)}) copy-start(bf16[768,1024]{1,0:T(8,128)(2,1)} %param.30) | copy-start | bytes 4718596
  1403.4 104.2 %copy-start.54 = (f32[768]{0:T(1024)S(1)}, f32[768]{0:T(1024)}, u32[]{:S(2)}) copy-start(f32[768]{0:T(1024)} %copy-done.53) | copy-start | bytes 9220
  1403.4 104.2 %copy-start.56 = (f32[1024]{0:T(1024)S(1)}, f32[1024]{0:T(1024)}, u32[]{:S(2)}) copy-start(f32[1024]{0:T(1024)} %copy-done.55) | copy-start | bytes 12292
  1405.0 105.2 %copy-start.59 = (f32[1024]{0:T(1024)S(1)}, f32[1024]{0:T(1024)}, u32[]{:S(2)}) copy-start(f32[1024]{0:T(1024)} %get-tuple-element.312) | copy-start | bytes 12292
  1405.0 216.7 %copy-start.50 = (f32[1024]{0:T(1024)S(1)}, f32[1024]{0:T(1024)}, u32[]{:S(2)}) copy-start(f32[1024]{0:T(1024)} %copy-done.49) | copy-start | bytes 12292
  1405.0 216.7 %copy-start.52 = (f32[768]{0:T(1024)S(1)}, f32[768]{0:T(1024)}, u32[]{:S(2)}) copy-start(f32[768]{0:T(1024)} %copy-done.51) | copy-start | bytes 9220
  1405.0 216.7 %copy-start.58 = (f32[768]{0:T(1024)S(1)}, f32[768]{0:T(1024)}, u32[]{:S(2)}) copy-start(f32[768]{0:T(1024)} %copy-done.57) | copy-start | bytes 9220
  (98 other events, 470.4 us)
Sparse Core Ops, SparseCore 0:
  13.6 118.0 all-gather.4
  330.6 210.0 reduce-scatter.4
  546.3 116.3 all-gather.6
  664.2 113.5 all-gather.8
  811.6 108.9 reduce-scatter.8
  928.5 115.8 all-gather.10
  1273.2 121.0 all-reduce.10
  1396.7 110.8 reduce-scatter.10
  1510.0 111.6 reduce-scatter.6
where the time goes:
time: 1640 us; the launch traced here: 1630 us
  waiting for transfers between devices  920 us (56%)
  matrix products  295 us (18%)
  local copies, waits for them, and re-layouts  233 us (14%)
  other arithmetic  137 us (8%)
  blocking collectives  31 us (2%)
    reduce_scatter x1, waiting for transfers between devices, on_device(): lax.psum_scatter(times_plain(lax.slice_in_dim(heads, 0, lax.axis_size('te...  210 us
    all_gather x1, waiting for transfers between devices, on_device(): lax.all_gather(normed_two.astype(jnp.bfloat16), 'tensor', axis=0, tiled=T...  116 us
    all_gather x1, waiting for transfers between devices, on_device(): lax.all_gather(normed_one.astype(jnp.bfloat16), 'tensor', axis=0, tiled=T...  111 us
    reduce_scatter x1, waiting for transfers between devices, on_device(): lax.psum_scatter((times_right(gate_piece, w_gate) + times_right(up_piece,...  109 us
    reduce_scatter x1, waiting for transfers between devices, on_device(): lax.psum_scatter((term + times_right(dv_low, value_matrix)).astype(jnp.bf...  100 us
    all_gather x1, waiting for transfers between devices, on_device(): grad_rows = lax.all_gather(out_grad, 'tensor', axis=0, tiled=True)  97.1 us
    all_gather x1, waiting for transfers between devices, on_device(): lax.all_gather(mid_grad.astype(jnp.bfloat16), 'tensor', axis=0, tiled=True)  90.2 us
    reduce_scatter x1, waiting for transfers between devices, on_device(): lax.psum_scatter(times_plain(lax.slice_in_dim(hidden, 0, lax.axis_size('t...  78 us
  transfers between devices with their start and end apart: 9, of which 9 were waited for; matrix products, arithmetic and copies ran while one was open for 11% of the time, Pallas kernels for 0%

commit v1 on v0

v1 whole, which is shorter than its diff:
```python
import functools
import math

import jax
import jax.numpy as jnp
from jax import lax
from jax.experimental import pallas as pl
from jax.experimental.pallas import tpu as pltpu
from jax.sharding import Mesh, PartitionSpec as P

SEQUENCE_TOKENS = 1024
HEAD = 128
epsilon = 1e-06
rope_base = 1000000.0
BF = jnp.bfloat16
F32 = jnp.float32
MIB = 1024 * 1024


def norm_forward(value, gain):
    inverse = lax.rsqrt(jnp.mean(value * value, axis=-1, keepdims=True) + epsilon)
    unit = value * inverse
    return (unit * gain, unit, inverse)


def norm_backward(grad, unit, inverse, gain):
    scaled = grad * gain
    back = inverse * (scaled - unit * jnp.mean(scaled * unit, axis=-1, keepdims=True))
    return back, grad * unit


def nn(left, right):
    return jnp.dot(left, right, preferred_element_type=F32)


def nt(left, right):
    return lax.dot_general(left, right, (((1,), (1,)), ((), ())), preferred_element_type=F32)


def tn(left, right):
    return lax.dot_general(left, right, (((0,), (0,)), ((), ())), preferred_element_type=F32)


def project(h_ref, w_ref, cos_ref, sin_ref, gq_ref, gk_ref, halo, qw):
    cos, sin = cos_ref[0], sin_ref[0]
    turn = lambda u, c, s: u * c + pltpu.roll(u, HEAD // 2, 1) * s
    kv = nn(h_ref[0], w_ref[0, :, qw:])
    kvw = kv.shape[1] // 2
    q_raw = nn(h_ref[0, halo:], w_ref[0, :, :qw])
    qs, ks = [], []
    for i in range(qw // HEAD):
        y, unit, inv = norm_forward(q_raw[:, i * HEAD : (i + 1) * HEAD], gq_ref[...])
        qs.append((turn(y, cos[halo:], sin[halo:]).astype(BF), unit, inv))
    for i in range(kvw // HEAD):
        y, unit, inv = norm_forward(kv[:, i * HEAD : (i + 1) * HEAD], gk_ref[...])
        v = kv[:, kvw + i * HEAD : kvw + (i + 1) * HEAD].astype(BF)
        ks.append((turn(y, cos, sin).astype(BF), unit, inv, v))
    return qs, ks


def attend_kernel(halo, block, qw, t_ref, h_ref, w_ref, cos_ref, sin_ref, gq_ref, gk_ref,
                  o_ref, l_ref, q_s, k_s, v_s, acc):
    qs, ks = project(h_ref, w_ref, cos_ref, sin_ref, gq_ref, gk_ref, halo, qw)
    rows = q_s.shape[0]
    group = len(qs) // len(ks)
    rate = HEAD**-0.5 * math.log2(math.e)
    whole = SEQUENCE_TOKENS // block
    first = t_ref[0] * (rows // block)
    low = lax.broadcasted_iota(jnp.int32, (block, block), 1) <= lax.broadcasted_iota(
        jnp.int32, (block, block), 0)
    for i, (q, _, _) in enumerate(qs):
        k, _, _, v = ks[i // group]
        q_s[...] = q
        if i % group == 0:
            k_s[...] = k
            v_s[...] = jnp.concatenate([v, jnp.ones_like(v)], axis=1)
        for b in range(rows // block):
            before = lax.rem(first + b, whole)
            qb = q_s[b * block : (b + 1) * block]
            own = halo + b * block
            s = nt(qb, k_s[own : own + block])
            e = jnp.where(low, jnp.exp2(s * rate), 0.0).astype(BF)
            acc[...] = nn(e, v_s[own : own + block])
            for j in range(1, whole):
                at = own - j * block
                if at < 0:
                    break

                @pl.when(before >= j)
                def _():
                    e = jnp.exp2(nt(qb, k_s[at : at + block]) * rate).astype(BF)
                    acc[...] += nn(e, v_s[at : at + block])

            inv = 1.0 / acc[:, HEAD:]
            o_ref[0, b * block : (b + 1) * block, i * HEAD : (i + 1) * HEAD] = (
                acc[:, :HEAD] * inv).astype(BF)
            l_ref[0, b * block : (b + 1) * block, i * HEAD : (i + 1) * HEAD] = inv


def attend_back_kernel(halo, block, qw, t_ref, h_ref, w_ref, cos_ref, sin_ref, gq_ref, gk_ref,
                       o_ref, l_ref, da_ref, wo_ref,
                       dq_ref, dkv_ref, share_ref, q_s, k_s, v_s, d_s, dq_s, dk_s, dv_s):
    qs, ks = project(h_ref, w_ref, cos_ref, sin_ref, gq_ref, gk_ref, halo, qw)
    rows, keys = q_s.shape[0], k_s.shape[0]
    group = len(qs) // len(ks)
    scale = HEAD**-0.5
    rate = scale * math.log2(math.e)
    whole = SEQUENCE_TOKENS // block
    first = t_ref[0] * (rows // block)
    high = lax.broadcasted_iota(jnp.int32, (block, block), 0) <= lax.broadcasted_iota(
        jnp.int32, (block, block), 1)
    cos, sin = cos_ref[0], sin_ref[0]
    back_turn = lambda g, c, s: g * c - pltpu.roll(g, HEAD // 2, 1) * s
    do = nt(da_ref[0], wo_ref[0]).astype(BF)
    kvw = len(ks) * HEAD
    share_q = jnp.zeros((1, HEAD), F32)
    share_k = jnp.zeros((1, HEAD), F32)
    for i, (q, unit_q, inv_q) in enumerate(qs):
        k, unit_k, inv_k, v = ks[i // group]
        at_head = slice(i * HEAD, (i + 1) * HEAD)
        q_s[...] = q
        if i % group == 0:
            k_s[...] = k
            lane = lax.broadcasted_iota(jnp.int32, (keys, HEAD), 1)
            v_s[...] = jnp.concatenate([v, jnp.where(lane < 2, 1.0, 0.0).astype(BF)], axis=1)
            dk_s[...] = jnp.zeros_like(dk_s)
            dv_s[...] = jnp.zeros_like(dv_s)
        d = (do[:, at_head].astype(F32) * l_ref[0, :, at_head]).astype(BF)
        delta = jnp.sum(d.astype(F32) * o_ref[0, :, at_head].astype(F32), axis=1, keepdims=True)
        upper = delta.astype(BF).astype(F32)
        lane = lax.broadcasted_iota(jnp.int32, (rows, HEAD), 1)
        extra = jnp.where(lane == 0, -upper, jnp.where(lane == 1, upper - delta, 0.0))
        d_s[...] = jnp.concatenate([d, extra.astype(BF)], axis=1)
        for b in range(rows // block):
            before = lax.rem(first + b, whole)
            qr = slice(b * block, (b + 1) * block)
            own = halo + b * block

            def part(at, masked):
                kr = slice(at, at + block)
                e = jnp.exp2(nt(k_s[kr], q_s[qr]) * rate)
                if masked:
                    e = jnp.where(high, e, 0.0)
                ds = (e * nt(v_s[kr], d_s[qr])).astype(BF)
                dv_s[kr] += nn(e.astype(BF), d_s[qr, :HEAD])
                dk_s[kr] += nn(ds, q_s[qr])
                return tn(ds, k_s[kr])

            dq_s[qr] = part(own, True)
            for j in range(1, whole):
                at = own - j * block
                if at < 0:
                    break

                @pl.when(before >= j)
                def _():
                    dq_s[qr] += part(at, False)

        grad = back_turn(dq_s[...] * scale, cos[halo:], sin[halo:])
        back, share = norm_backward(grad, unit_q, inv_q, gq_ref[...])
        share_q += jnp.sum(share, axis=0, keepdims=True)
        dq_ref[0, 0, :, at_head] = back.astype(BF)
        if i % group == group - 1:
            kh = i // group
            grad = back_turn(dk_s[...] * scale, cos, sin)
            back, share = norm_backward(grad, unit_k, inv_k, gk_ref[...])
            share_k += jnp.sum(share, axis=0, keepdims=True)
            dkv_ref[0, 0, :, kh * HEAD : (kh + 1) * HEAD] = back.astype(BF)
            dkv_ref[0, 0, :, kvw + kh * HEAD : kvw + (kh + 1) * HEAD] = dv_s[...].astype(BF)
    share_ref[0, 0] = jnp.concatenate(
        [share_q, share_k, jnp.zeros((6, HEAD), F32)], axis=0)


def attention_specs(keys, width, qkv, tensor):
    return [
        pl.BlockSpec(memory_space=pltpu.SMEM),
        pl.BlockSpec((1, keys, width), lambda s, t: (s, 0, 0)),
        pl.BlockSpec((1, width, qkv), lambda s, t: (t, 0, 0)),
        pl.BlockSpec((1, keys, HEAD), lambda s, t: (s, 0, 0)),
        pl.BlockSpec((1, keys, HEAD), lambda s, t: (s, 0, 0)),
        pl.BlockSpec((1, HEAD), lambda s, t: (0, 0)),
        pl.BlockSpec((1, HEAD), lambda s, t: (0, 0)),
    ]


def attend(block, halo, qw, t, h1, wqkv, cos, sin, gq, gk):
    split, keys, width = h1.shape
    tensor, _, qkv = wqkv.shape
    rows = keys - halo
    head_block = pl.BlockSpec((1, rows, qw), lambda s, t: (s, 0, t))
    return pl.pallas_call(
        functools.partial(attend_kernel, halo, block, qw),
        grid=(split, tensor),
        in_specs=attention_specs(keys, width, qkv, tensor),
        out_specs=[head_block, head_block],
        out_shape=[
            jax.ShapeDtypeStruct((split, rows, tensor * qw), BF),
            jax.ShapeDtypeStruct((split, rows, tensor * qw), F32),
        ],
        scratch_shapes=[
            pltpu.VMEM((rows, HEAD), BF),
            pltpu.VMEM((keys, HEAD), BF),
            pltpu.VMEM((keys, 2 * HEAD), BF),
            pltpu.VMEM((block, 2 * HEAD), F32),
        ],
        cost_estimate=pl.CostEstimate(
            flops=60_000_000_000, bytes_accessed=30_000_000, transcendentals=10_000_000),
        compiler_params=pltpu.CompilerParams(vmem_limit_bytes=48 * MIB),
    )(t, h1, wqkv, cos, sin, gq, gk)


def attend_back(block, halo, qw, t, h1, wqkv, cos, sin, gq, gk, o, l, da, wo):
    split, keys, width = h1.shape
    tensor, _, qkv = wqkv.shape
    rows = keys - halo
    head_block = pl.BlockSpec((1, rows, qw), lambda s, t: (s, 0, t))
    return pl.pallas_call(
        functools.partial(attend_back_kernel, halo, block, qw),
        grid=(split, tensor),
        in_specs=attention_specs(keys, width, qkv, tensor)
        + [
            head_block,
            head_block,
            pl.BlockSpec((1, rows, width), lambda s, t: (s, 0, 0)),
            pl.BlockSpec((1, qw, width), lambda s, t: (t, 0, 0)),
        ],
        out_specs=[
            pl.BlockSpec((1, 1, rows, qw), lambda s, t: (t, s, 0, 0)),
            pl.BlockSpec((1, 1, keys, qkv - qw), lambda s, t: (t, s, 0, 0)),
            pl.BlockSpec((1, 1, 8, HEAD), lambda s, t: (t, s, 0, 0)),
        ],
        out_shape=[
            jax.ShapeDtypeStruct((tensor, split, rows, qw), BF),
            jax.ShapeDtypeStruct((tensor, split, keys, qkv - qw), BF),
            jax.ShapeDtypeStruct((tensor, split, 8, HEAD), F32),
        ],
        scratch_shapes=[
            pltpu.VMEM((rows, HEAD), BF),
            pltpu.VMEM((keys, HEAD), BF),
            pltpu.VMEM((keys, 2 * HEAD), BF),
            pltpu.VMEM((rows, 2 * HEAD), BF),
            pltpu.VMEM((rows, HEAD), F32),
            pltpu.VMEM((keys, HEAD), F32),
            pltpu.VMEM((keys, HEAD), F32),
        ],
        cost_estimate=pl.CostEstimate(
            flops=120_000_000_000, bytes_accessed=40_000_000, transcendentals=10_000_000),
        compiler_params=pltpu.CompilerParams(vmem_limit_bytes=56 * MIB),
    )(t, h1, wqkv, cos, sin, gq, gk, o, l, da, wo)


def feed_kernel(chunk, h_ref, ht_ref, dy_ref, wgu_ref, wd_ref,
                y_ref, dh_ref, dgu_ref, dwd_ref, hid_s, dg_s, du_s):
    rows = h_ref.shape[0]
    width = wd_ref.shape[1]

    @pl.when(pl.program_id(0) == 0)
    def _():
        y_ref[...] = jnp.zeros_like(y_ref)
        dh_ref[...] = jnp.zeros_like(dh_ref)

    for c in range(rows // chunk):
        at = slice(c * chunk, (c + 1) * chunk)
        gate = nn(h_ref[at], wgu_ref[0, :, :width])
        up = nn(h_ref[at], wgu_ref[0, :, width:])
        dhid = nt(dy_ref[at], wd_ref[0])
        sigma = 1.0 / (1.0 + jnp.exp(-gate))
        act = gate * sigma
        hid_s[at] = (act * up).astype(BF)
        du_s[at] = (dhid * act).astype(BF)
        dg_s[at] = (dhid * up * (sigma + act * (1.0 - sigma))).astype(BF)
        y_ref[at] += nn(hid_s[at], wd_ref[0])
        dh_ref[at] += nt(dg_s[at], wgu_ref[0, :, :width]) + nt(du_s[at], wgu_ref[0, :, width:])
    dgu_ref[0, :, :width] = nn(ht_ref[...], dg_s[...]).astype(BF)
    dgu_ref[0, :, width:] = nn(ht_ref[...], du_s[...]).astype(BF)
    dwd_ref[0] = tn(hid_s[...], dy_ref[...]).astype(BF)


def feed(h2, dy, wgu, wd):
    rows, model = h2.shape
    tensor, _, two = wgu.shape
    width = two // 2
    whole = pl.BlockSpec(memory_space=pltpu.VMEM)
    return pl.pallas_call(
        functools.partial(feed_kernel, rows // max(1, rows // 512)),
        grid=(tensor,),
        in_specs=[
            whole, whole, whole,
            pl.BlockSpec((1, model, two), lambda t: (t, 0, 0)),
            pl.BlockSpec((1, width, model), lambda t: (t, 0, 0)),
        ],
        out_specs=[
            whole, whole,
            pl.BlockSpec((1, model, two), lambda t: (t, 0, 0)),
            pl.BlockSpec((1, width, model), lambda t: (t, 0, 0)),
        ],
        out_shape=[
            jax.ShapeDtypeStruct((rows, model), F32),
            jax.ShapeDtypeStruct((rows, model), F32),
            jax.ShapeDtypeStruct((tensor, model, two), BF),
            jax.ShapeDtypeStruct((tensor, width, model), BF),
        ],
        scratch_shapes=[pltpu.VMEM((rows, width), BF)] * 3,
        cost_estimate=pl.CostEstimate(
            flops=50_000_000_000, bytes_accessed=40_000_000, transcendentals=3_000_000),
        compiler_params=pltpu.CompilerParams(vmem_limit_bytes=58 * MIB),
    )(h2, h2.T, dy, wgu, wd)


def on_device(pairs, split, tensor, tokens, positions, first_gain, w_query, key_matrix,
              value_matrix, query_gain, key_gain, w_output, second_gain, w_gate, w_up, w_down,
              out_grad):
    rows, model = tokens.shape
    pair, core, t = lax.axis_index("pair"), lax.axis_index("core"), lax.axis_index("tensor")
    hops = max(-(-(d * rows % SEQUENCE_TOKENS) // rows) for d in range(tensor))
    halo = hops * rows
    block = math.gcd(rows, 256)
    keys = halo + rows
    spread, home = ("tensor", "pair"), ("pair", "core")

    def other(value):
        return lax.ppermute(value, "core", [(0, 1), (1, 0)])

    def both(value):
        return jnp.stack([value, other(value)]) if split == 2 else value[None]

    def own_sum(parts):
        return parts[0] + other(parts[1].astype(BF)).astype(F32) if split == 2 else parts[0]

    def columns(w):
        cols, deep = w.shape[1] // split, w.shape[0] // pairs
        return lax.dynamic_slice(w, (pair * deep, core * cols), (deep, cols))

    def lines(w):
        deep = w.shape[0] // (split * pairs)
        return lax.dynamic_slice_in_dim(w, (core * pairs + pair) * deep, deep, 0)

    def gather(w):
        return lax.all_gather(w, spread, axis=0, tiled=True)

    reach = [
        lax.ppermute(tokens, "tensor", [(d, d + h) for d in range(tensor - h)])
        for h in range(hops, 0, -1)
    ]
    wqkv = gather(jnp.concatenate([columns(w_query), columns(key_matrix), columns(value_matrix)], 1))
    wqkv = wqkv.reshape(tensor, model, -1)
    qw = w_query.shape[1] // split
    wo = gather(lines(w_output)).reshape(tensor, qw, model)
    wgu = gather(jnp.concatenate([columns(w_gate), columns(w_up)], 1)).reshape(tensor, model, -1)
    wd = gather(lines(w_down)).reshape(tensor, -1, model)

    gain_one = first_gain.astype(F32)
    gain_two = second_gain.astype(F32)
    gq = query_gain.astype(F32)[None]
    gk = key_gain.astype(F32)[None]
    rate = jnp.exp(-math.log(rope_base) * 2.0 * jnp.arange(HEAD // 2, dtype=F32) / HEAD)
    place = jnp.concatenate([jnp.zeros((halo,), F32), positions.astype(F32)])
    place = both(lax.dynamic_slice_in_dim(place, t * rows, keys, 0))
    angles = place[..., None] * rate
    cosine, sine = jnp.cos(angles), jnp.sin(angles)
    cos = jnp.concatenate([cosine, cosine], axis=-1)
    sin = jnp.concatenate([-sine, sine], axis=-1)
    t_ref = t[None].astype(jnp.int32)

    resid = tokens.astype(F32)
    _, unit_one, inv_one = norm_forward(resid, gain_one)
    seen = both(jnp.concatenate(reach + [tokens], axis=0))
    h1 = norm_forward(seen.astype(F32), gain_one)[0].astype(BF)
    grads = both(out_grad)
    o, l = attend(block, halo, qw, t_ref, h1, wqkv, cos, sin, gq, gk)
    o_rows = o.reshape(split * rows, -1)
    wo_flat = wo.reshape(-1, model)
    mid = resid + own_sum(nn(o_rows, wo_flat).reshape(split, rows, model))
    normed_two, unit_two, inv_two = norm_forward(mid, gain_two)
    h2 = both(normed_two.astype(BF)).reshape(split * rows, model)
    y, dh2, dgu, dwd = feed(h2, grads.reshape(split * rows, model), wgu, wd)
    layer_out = (mid + own_sum(y.reshape(split, rows, model))).astype(BF)
    dh2 = own_sum(dh2.reshape(split, rows, model))
    back_two, share_two = norm_backward(dh2, unit_two, inv_two, gain_two)
    mid_grad = out_grad.astype(F32) + back_two
    da = both(mid_grad.astype(BF))
    dwo = tn(o_rows, da.reshape(split * rows, model)).astype(BF)
    dq, dkv, shares = attend_back(
        block, halo, qw, t_ref, h1, wqkv, cos, sin, gq, gk, o, l, da, wo)

    dh_kv = jnp.zeros((split * keys, model), F32)
    dh_q = jnp.zeros((split * rows, model), F32)
    h_rows = h1[:, halo:].reshape(split * rows, model)
    h_keys = h1.reshape(split * keys, model)
    terms = []
    for d in range(tensor):
        dq_d = dq[d].reshape(split * rows, -1)
        dkv_d = dkv[d].reshape(split * keys, -1)
        dh_kv += nt(dkv_d, wqkv[d, :, qw:])
        dh_q += nt(dq_d, wqkv[d, :, :qw])
        terms.append(jnp.concatenate([tn(h_rows, dq_d), tn(h_keys, dkv_d)], axis=1).astype(BF))
    dh_kv = dh_kv.reshape(split, keys, model)
    dh_own = own_sum(dh_kv[:, halo:] + dh_q.reshape(split, rows, model))
    if hops:
        dh_far = own_sum(dh_kv[:, :halo]).astype(BF)
        for h in range(hops, 0, -1):
            at = (hops - h) * rows
            dh_own += lax.ppermute(
                dh_far[at : at + rows], "tensor", [(d + h, d) for d in range(tensor - h)]
            ).astype(F32)
    back_one, share_one = norm_backward(dh_own, unit_one, inv_one, gain_one)
    input_grad = (mid_grad + back_one).astype(BF)

    def reduce(w):
        return lax.psum_scatter(w.reshape(-1, w.shape[-1]), spread, scatter_dimension=0, tiled=True)

    def from_columns(w):
        deep, cols = w.shape
        w = lax.all_gather(w, home, axis=0, tiled=True).reshape(pairs, split, deep, cols)
        return w

    def join(w, start, cols):
        w = w[..., start : start + cols]
        return w.transpose(0, 2, 1, 3).reshape(model, split * cols).astype(F32)

    def from_lines(w):
        return lax.all_gather(w, ("core", "pair"), axis=0, tiled=True).astype(F32)

    gu = from_columns(reduce(dgu))
    down_wgrad = from_lines(reduce(dwd))
    out_wgrad = from_lines(reduce(dwo))
    qkv = from_columns(reduce(jnp.stack(terms)))
    fw = gu.shape[-1] // 2
    kw = (qkv.shape[-1] - qw) // 2
    shares = jnp.sum(shares, axis=(0, 1))
    gains = jnp.concatenate(
        [jnp.sum(share_one, axis=0), jnp.sum(share_two, axis=0), shares[0], shares[1]])
    gains = lax.psum(gains, ("pair", "core", "tensor"))

    def piece(start, size):
        return lax.dynamic_slice_in_dim(gains, start + t * (size // tensor), size // tensor, 0)

    return (
        layer_out,
        input_grad,
        piece(0, model),
        join(qkv, 0, qw),
        join(qkv, qw, kw),
        join(qkv, qw + kw, kw),
        piece(2 * model, HEAD),
        piece(2 * model + HEAD, HEAD),
        out_wgrad,
        piece(model, model),
        join(gu, 0, fw),
        join(gu, fw, fw),
        down_wgrad,
    )


def solution(mesh):
    dp, tensor = mesh.shape["dp"], mesh.shape["tensor"]

    def run(*args):
        heads = args[4].shape[1] // HEAD // tensor
        split = 2 if dp % 2 == 0 and heads % 2 == 0 else 1
        fine = Mesh(mesh.devices.reshape(dp // split, split, tensor), ("pair", "core", "tensor"))
        token = P(("pair", "core", "tensor"), None)
        column, line, copied = P(None, "tensor"), P("tensor", None), P()
        return jax.shard_map(
            functools.partial(on_device, dp // split, split, tensor),
            mesh=fine,
            in_specs=(token, P(("pair", "core")), copied, column, column, column, copied, copied,
                      line, copied, column, column, line, token),
            out_specs=(token, token, P("tensor"), column, column, column, P("tensor"),
                       P("tensor"), line, P("tensor"), column, column, line),
            check_vma=False,
        )(*args)

    return run
```

time: 1640 us -> 1020 us (0.62)
  waiting for transfers between devices: 920 us -> 497 us
  Pallas kernels: 0 us -> 230 us
  matrix products: 295 us -> 91.6 us
  local copies, waits for them, and re-layouts: 233 us -> 57.8 us
  other arithmetic: 137 us -> 69 us
    all_gather x4 -> x8, waiting for transfers between devices: 414 us -> 140 us  [the longest x4 140 us: gather(): return lax.all_gather(w, spread, axis=0, tiled=True)]
    reduce_scatter x4, waiting for transfers between devices: 497 us -> 260 us  [reduce(): lax.psum_scatter(w.reshape(-1, w.shape[-1]), spread, scatter_dimension=0,...]
    pallas_call x0 -> x3, Pallas kernels: none -> 230 us  [the longest x1 94.9 us: attend_back(): pl.pallas_call(functools.partial(attend_back_kernel, halo, block, qw), gr...]
    dot_general x63 -> x18, matrix products: 295 us -> 91.6 us  [the longest x8 63.2 us: nt(): lax.dot_general(left, right, (((1,), (1,)), ((), ())), preferred_element_...]
    ppermute x0 -> x12, waiting for transfers between devices: none -> 95.3 us  [the longest x1 50.6 us: on_device(): lax.ppermute(tokens, 'tensor', [(d, d + h) for d in range(tensor - h)])]
    reshape x7 -> x1, local copies, waits for them, and re-layouts: 48.1 us -> 4.79 us  [on_device(): h2 = both(normed_two.astype(BF)).reshape(split * rows, model)]
    dynamic_update_slice x18 -> x0, local copies, waits for them, and re-layouts: 41.1 us -> none  [the longest x12 26.2 us: on_device(): lax.map(seq_backward, (q_five, k_four, v_four, grad_five, log_sums))]
    while x80 -> x0, local copies, waits for them, and re-layouts: 32.6 us -> none
  transfers between devices with their start and end apart: 9 -> 24, of which waited for: 9 -> 15; matrix products, arithmetic and copies ran while one was open for 11% -> 19% of each run, Pallas kernels for 0% -> 16%
where the time goes in v1:
time: 1020 us; the launch traced here: 1010 us
  waiting for transfers between devices  497 us (49%)
  Pallas kernels  230 us (23%)
  matrix products  91.6 us (9%)
  other arithmetic  69 us (7%)
  local copies, waits for them, and re-layouts  57.8 us (6%)
  blocking collectives  40.3 us (4%)
  between operations  15.4 us (2%)
    reduce_scatter x4, waiting for transfers between devices, reduce(): lax.psum_scatter(w.reshape(-1, w.shape[-1]), spread, scatter_dimension=0,...  260 us
    all_gather x4, waiting for transfers between devices, gather(): return lax.all_gather(w, spread, axis=0, tiled=True)  140 us
    pallas_call x1, Pallas kernels, attend_back(): pl.pallas_call(functools.partial(attend_back_kernel, halo, block, qw), gr...  94.9 us
    pallas_call x1, Pallas kernels, attend(): pl.pallas_call(functools.partial(attend_kernel, halo, block, qw), grid=(s...  70.6 us
    pallas_call x1, Pallas kernels, feed(): pl.pallas_call(functools.partial(feed_kernel, rows // max(1, rows // 512)...  64.7 us
    dot_general x8, matrix products, nt(): lax.dot_general(left, right, (((1,), (1,)), ((), ())), preferred_element_...  63.2 us
    ppermute x1, waiting for transfers between devices, on_device(): lax.ppermute(tokens, 'tensor', [(d, d + h) for d in range(tensor - h)])  50.6 us
    psum x1, blocking collectives, on_device(): gains = lax.psum(gains, ('pair', 'core', 'tensor'))  40.3 us
  transfers between devices with their start and end apart: 24, of which 15 were waited for; matrix products, arithmetic and copies ran while one was open for 19% of the time, Pallas kernels for 16%

profile of v1, /device:TPU:0, one launch (start us, length us, event | category | flops | bytes accessed | tf_op | source)
XLA Modules:
  0.0 1009.7 jit_solution(374432773624220996)
XLA Ops:
  13.3 5.0 collective-permute-start
  18.3 50.6 %collective-permute-done = bf16[768,1024]{1,0:T(8,128)(2,1)S(1)} collective-permute-done((bf16[768,1024]{1,0:T(8,128)(2,1)}, bf16[768,1024]{1,0:T(8,128)(2,1)S(1)}, u32[]{:S(2)}, u32[]{:S(2)}) %collective-permute-start) | collective-permute-done | bytes 1572896 | tf_op jit(solution)/shard_map/ppermute | solution.py:342
  76.8 5.7 fusion.33
  83.4 5.2 fusion
  88.7 7.1 fusion.2.h_ref
  99.4 70.6 %shard_map.237 = (bf16[2,768,1024]{2,1,0:T(8,128)(2,1)}, f32[2,768,1024]{2,1,0:T(8,128)}) custom-call(s32[1]{0:T(128)} %bitcast.t_ref, bf16[2,1536,1024]{2,1,0:T(8,128)(2,1)} %fusion.2.h_ref, bf16[4,1024,512]{2,1,0:T(8,128)(2,1)} %bitcast.197, f32[2,1536,128]{2,1,0:T(8,128)S(1)} %get-tuple-element.62.cos_ref, f32[2,1536,128]{2,1,0:T(8,128)S(1)} %get-tuple-element.63.sin_ref, ...), custom_call_target="tpu_custom_call" | custom-call | flops 60000002048 | bytes 30000000 | tf_op jit(solution)/shard_map/pallas_call | solution.py:191
  170.0 6.1 fusion.39
  187.1 4.8 copy.36
  191.9 40.7 %all-gather.15.cloned.1.call-done = bf16[1536,1024]{1,0:T(8,128)(2,1)} async-done(((bf16[96,1024]{1,0:T(8,128)(2,1)}), bf16[1536,1024]{1,0:T(8,128)(2,1)}) %all-gather.15.cloned.1.call-update) | async-done | bytes 3145744 | tf_op jit(solution)/shard_map/all_gather | solution.py:339
  232.6 95.9 %all-gather.13.cloned.1.call-done = bf16[4096,768]{1,0:T(8,128)(2,1)} async-done(((bf16[256,768]{1,0:T(8,128)(2,1)}), bf16[4096,768]{1,0:T(8,128)(2,1)}) %all-gather.13.cloned.1.call-update) | async-done | bytes 6291472 | tf_op jit(solution)/shard_map/all_gather | solution.py:339
  328.5 64.7 %shard_map.238 = (f32[1536,1024]{1,0:T(8,128)}, f32[1536,1024]{1,0:T(8,128)}, bf16[4,1024,768]{2,1,0:T(8,128)(2,1)}, bf16[4,384,1024]{2,1,0:T(8,128)(2,1)}) custom-call(bf16[1536,1024]{1,0:T(8,128)(2,1)} %bitcast.177, bf16[1024,1536]{1,0:T(8,128)(2,1)} %bitcast.219, bf16[1536,1024]{1,0:T(8,128)(2,1)} %bitcast.218, bf16[4,1024,768]{2,1,0:T(8,128)(2,1)} %bitcast.230, ...), custom_call_target="tpu_custom_call" | custom-call | flops 49999998976 | bytes 40000000 | tf_op jit(solution)/shard_map/pallas_call | solution.py:284
  412.1 94.9 %shard_map.239 = (bf16[4,2,768,256]{3,2,1,0:T(8,128)(2,1)}, bf16[4,2,1536,256]{3,2,1,0:T(8,128)(2,1)}, f32[4,2,8,128]{3,2,1,0:T(8,128)}) custom-call(s32[1]{0:T(128)} %bitcast.t_ref, bf16[2,1536,1024]{2,1,0:T(8,128)(2,1)} %fusion.2.h_ref, bf16[4,1024,512]{2,1,0:T(8,128)(2,1)} %bitcast.198, f32[2,1536,128]{2,1,0:T(8,128)} %copy-done.2, ...), custom_call_target="tpu_custom_call" | custom-call | flops 120000004096 | bytes 40000000 | tf_op jit(solution)/shard_map/pallas_call | solution.py:217
  515.5 6.1 bitcast_convert_fusion
  535.9 5.1 maximum_maximum_fusion
  541.0 6.2 copy.37
  548.8 74.5 %reduce-scatter.7.cloned.1.call-done = bf16[64,1024]{1,0:T(8,128)(2,1)} async-done(((bf16[1024,1024]{1,0:T(8,128)(2,1)}), bf16[64,1024]{1,0:T(8,128)(2,1)}) %reduce-scatter.7.cloned.1.call-update) | async-done | bytes 131088 | tf_op jit(solution)/shard_map/reduce_scatter | solution.py:410
  623.6 7.9 fusion.31
  631.5 7.5 fusion.32
  639.0 79.1 %reduce-scatter.5.cloned.1.call-done = bf16[256,512]{1,0:T(8,128)(2,1)} async-done(((bf16[4096,512]{1,0:T(8,128)(2,1)}), bf16[256,512]{1,0:T(8,128)(2,1)}) %reduce-scatter.5.cloned.1.call-update) | async-done | bytes 262160 | tf_op jit(solution)/shard_map/reduce_scatter | solution.py:410
  718.1 7.6 fusion.30
  725.7 18.3 %add_add_fusion = f32[3072,1024]{1,0:T(8,128)} fusion(f32[3072,1024]{1,0:T(8,128)} %fusion.30, f32[3072,1024]{1,0:T(8,128)} %fusion.32, f32[3072,1024]{1,0:T(8,128)} %fusion.31, bf16[3072,256]{1,0:T(8,128)(2,1)S(1)} %bitcast.188, bf16[4,1024,512]{2,1,0:T(8,128)(2,1)} %bitcast.202), kind=kOutput, calls=%fused_computation.5 | convolution fusion | flops 1620049920 | bytes 52428800 | tf_op jit(solution)/shard_map/dot_general | solution.py:37
  747.5 4.8 fusion.27
  752.3 4.7 fusion.28
  757.0 4.9 fusion.29
  761.8 106.6 %reduce-scatter.9.cloned.1.call-done = bf16[256,768]{1,0:T(8,128)(2,1)} async-done(((bf16[4096,768]{1,0:T(8,128)(2,1)}), bf16[256,768]{1,0:T(8,128)(2,1)}) %reduce-scatter.9.cloned.1.call-update) | async-done | bytes 393232 | tf_op jit(solution)/shard_map/reduce_scatter | solution.py:410
  868.5 7.6 add_add_fusion.1
  876.1 4.4 slice_add_fusion
  882.1 5.2 fusion.14
  888.7 36.4 %collective-permute-done.11 = bf16[768,1024]{1,0:T(8,128)(2,1)} collective-permute-done((bf16[768,1024]{1,0:T(8,128)(2,1)}, bf16[768,1024]{1,0:T(8,128)(2,1)}, u32[]{:S(2)}, u32[]{:S(2)}) %collective-permute-start.11) | collective-permute-done | bytes 1572896 | tf_op jit(solution)/shard_map/ppermute | solution.py:403
  925.2 3.6 fusion.11
  928.8 40.3 %psum.7 = f32[2304]{0:T(1024)S(1)} all-reduce(f32[2304]{0:T(1024)S(1)} %pad_maximum_fusion.9), channel_id=1, replica_groups=mesh['pair'=4,'core'=2,'tensor'=4] {'pair','core','tensor'}, use_global_device_ids=true, to_apply=%region_8.0 | all-reduce | flops 2304 | bytes 18432 | tf_op jit(solution)/shard_map/psum | solution.py:433
  970.3 5.2 fusion.10
  (214 shorter events, 107.0 us)
Async XLA Ops:
  7.2 63.0 %copy-start.7 = (bf16[768,1024]{1,0:T(8,128)(2,1)S(1)}, bf16[768,1024]{1,0:T(8,128)(2,1)}, u32[]{:S(2)}) copy-start(bf16[768,1024]{1,0:T(8,128)(2,1)} %param.14) | copy-start | bytes 4718596
  7.2 92.2 %all-gather.9.cloned.1.call-start = ((), (), s32[]{:S(2)}) async-start(), calls=%async_computation.4 | async-start | bytes 4456448 | tf_op jit(solution)/shard_map/all_gather | solution.py:339
  10.8 159.2 %all-gather.11.cloned.1.call-start = ((), (), s32[]{:S(2)}) async-start(), calls=%async_computation.5 | async-start | bytes 2228224 | tf_op jit(solution)/shard_map/all_gather | solution.py:339
  12.4 220.2 %all-gather.15.cloned.1.call-start = ((), (), s32[]{:S(2)}) async-start(), calls=%async_computation.7 | async-start | bytes 3342336 | tf_op jit(solution)/shard_map/all_gather | solution.py:339
  13.2 58.3 %copy-start.35 = (s32[3072]{0:T(1024)S(1)}, s32[3072]{0:T(1024)}, u32[]{:S(2)}) copy-start(s32[3072]{0:T(1024)} %param.15) | copy-start | bytes 36868
  13.2 315.3 %all-gather.13.cloned.1.call-start = ((), (), s32[]{:S(2)}) async-start(), calls=%async_computation.6 | async-start | bytes 6684672 | tf_op jit(solution)/shard_map/all_gather | solution.py:339
  13.3 55.7 %collective-permute-start = (bf16[768,1024]{1,0:T(8,128)(2,1)}, bf16[768,1024]{1,0:T(8,128)(2,1)S(1)}, u32[]{:S(2)}, u32[]{:S(2)}) collective-permute-start(bf16[768,1024]{1,0:T(8,128)(2,1)} %param.14), channel_id=1, source_target_pairs={{0,1},{1,2},{2,3},{4,5},{5,6},{6,7},{8,9},{9,10},{10,11},{12,13},{... | collective-permute-start | bytes 4718600 | tf_op jit(solution)/shard_map/ppermute | solution.py:342
  71.5 11.9 %collective-permute-start.1 = (bf16[1536,1024]{1,0:T(8,128)(2,1)}, bf16[1536,1024]{1,0:T(8,128)(2,1)}, u32[]{:S(2)}, u32[]{:S(2)}) collective-permute-start(bf16[1536,1024]{1,0:T(8,128)(2,1)} %constant_dynamic-update-slice_fusion), channel_id=1, source_target_pairs={{0,4},{4,0},{1,5},{5,1},{2,6},{6,2},{3,7},{7,3},{8,12},{12,8},{9,1... | collective-permute-start | bytes 9437192 | tf_op jit(solution)/shard_map/ppermute | solution.py:322
  71.6 5.2 collective-permute-start.2
  74.8 473.3 %reduce-scatter.11.cloned.1.call-start = ((), (), s32[]{:S(2)}) async-start(), calls=%async_computation.14 | async-start | bytes 3342336 | tf_op jit(solution)/shard_map/reduce_scatter | solution.py:410
  74.9 24.5 %copy-start.4 = (f32[1,128]{1,0:T(1,128)}, f32[1,128]{1,0:T(1,128)S(1)}, u32[]{:S(2)}) copy-start(f32[1,128]{1,0:T(1,128)S(1)} %get-tuple-element.64.gk_ref) | copy-start | bytes 1540
  74.9 24.5 %copy-start.5 = (f32[1,128]{1,0:T(1,128)}, f32[1,128]{1,0:T(1,128)S(1)}, u32[]{:S(2)}) copy-start(f32[1,128]{1,0:T(1,128)S(1)} %get-tuple-element.65.gq_ref) | copy-start | bytes 1540
  176.4 3.5 collective-permute-start.3
  177.6 4.6 collective-permute-start.5
  181.7 3.5 collective-permute-start.4
  395.5 3.5 collective-permute-start.7
  398.1 3.5 collective-permute-start.6
  405.1 3.6 collective-permute-start.8
  407.3 216.1 %reduce-scatter.7.cloned.1.call-start = ((), (), s32[]{:S(2)}) async-start(), calls=%async_computation.10 | async-start | bytes 2228224 | tf_op jit(solution)/shard_map/reduce_scatter | solution.py:410
  521.6 196.4 %reduce-scatter.5.cloned.1.call-start = ((), (), s32[]{:S(2)}) async-start(), calls=%async_computation.8 | async-start | bytes 4456448 | tf_op jit(solution)/shard_map/reduce_scatter | solution.py:410
  547.3 321.1 %reduce-scatter.9.cloned.1.call-start = ((), (), s32[]{:S(2)}) async-start(), calls=%async_computation.12 | async-start | bytes 6684672 | tf_op jit(solution)/shard_map/reduce_scatter | solution.py:410
  548.1 427.5 %all-gather.23.cloned.1.call-start = ((), (), s32[]{:S(2)}) async-start(), calls=%async_computation.15 | async-start | bytes 1769472 | tf_op jit(solution)/shard_map/all_gather | solution.py:422
  548.8 430.2 %all-gather.19.cloned.1.call-start = ((), (), s32[]{:S(2)}) async-start(), calls=%async_computation.11 | async-start | bytes 1179648 | tf_op jit(solution)/shard_map/all_gather | solution.py:422
  623.4 358.4 %all-gather.17.cloned.1.call-start = ((), (), s32[]{:S(2)}) async-start(), calls=%async_computation.9 | async-start | bytes 2359296 | tf_op jit(solution)/shard_map/all_gather | solution.py:414
  718.1 273.1 %all-gather.21.cloned.1.call-start = ((), (), s32[]{:S(2)}) async-start(), calls=%async_computation.13 | async-start | bytes 3538944 | tf_op jit(solution)/shard_map/all_gather | solution.py:414
  747.5 134.6 %collective-permute-start.10 = (bf16[768,1024]{1,0:T(8,128)(2,1)}, bf16[768,1024]{1,0:T(8,128)(2,1)}, u32[]{:S(2)}, u32[]{:S(2)}) collective-permute-start(bf16[768,1024]{1,0:T(8,128)(2,1)} %fusion.18), channel_id=1, source_target_pairs={{0,4},{4,0},{1,5},{5,1},{2,6},{6,2},{3,7},{7,3},{8,12},{12,8},{9,1... | collective-permute-start | bytes 4718600 | tf_op jit(solution)/shard_map/ppermute | solution.py:322
  757.0 111.5 %copy-start.24 = (bf16[1,2,768,256]{3,2,1,0:T(8,128)(2,1)S(1)}, bf16[1,2,768,256]{3,2,1,0:T(8,128)(2,1)}, u32[]{:S(2)}) copy-start(bf16[1,2,768,256]{3,2,1,0:T(8,128)(2,1)} %copy-done.23) | copy-start | bytes 2359300
  882.0 43.2 %copy-start.9 = (bf16[768,1024]{1,0:T(8,128)(2,1)S(1)}, bf16[768,1024]{1,0:T(8,128)(2,1)}, u32[]{:S(2)}) copy-start(bf16[768,1024]{1,0:T(8,128)(2,1)} %param.14) | copy-start | bytes 4718596
  882.0 43.2 %copy-start.31 = (f32[1024]{0:T(1024)S(1)}, f32[1024]{0:T(1024)}, u32[]{:S(2)}) copy-start(f32[1024]{0:T(1024)} %copy-done.30) | copy-start | bytes 12292
  882.0 6.7 collective-permute-start.9
  887.3 37.8 %collective-permute-start.11 = (bf16[768,1024]{1,0:T(8,128)(2,1)}, bf16[768,1024]{1,0:T(8,128)(2,1)}, u32[]{:S(2)}, u32[]{:S(2)}) collective-permute-start(bf16[768,1024]{1,0:T(8,128)(2,1)} %fusion.14), channel_id=1, source_target_pairs={{1,0},{2,1},{3,2},{5,4},{6,5},{7,6},{9,8},{10,9},{11,10},{13,12},{... | collective-permute-start | bytes 4718600 | tf_op jit(solution)/shard_map/ppermute | solution.py:403
  888.7 40.1 %copy-start.34 = (f32[1024]{0:T(1024)S(1)}, f32[1024]{0:T(1024)}, u32[]{:S(2)}) copy-start(f32[1024]{0:T(1024)} %get-tuple-element.33) | copy-start | bytes 12292
  (37 other events, 198.8 us)
Sparse Core Ops, SparseCore 0:
  11.4 87.9 all-gather.8
  102.7 59.9 all-gather.10
  166.1 66.4 all-gather.14
  235.8 92.6 all-gather.12
  407.4 128.8 reduce-scatter.10
  539.0 84.3 reduce-scatter.6
  625.6 92.3 reduce-scatter.4
  723.3 145.0 reduce-scatter.8
  870.3 24.7 all-gather.22
  896.9 23.4 all-gather.18
  922.3 28.4 all-gather.16
  952.5 32.8 all-gather.20

commit v2 on v1

--- a/solution.py
+++ b/solution.py
@@ -345,9 +345,14 @@
     wqkv = gather(jnp.concatenate([columns(w_query), columns(key_matrix), columns(value_matrix)], 1))
     wqkv = wqkv.reshape(tensor, model, -1)
     qw = w_query.shape[1] // split
-    wo = gather(lines(w_output)).reshape(tensor, qw, model)
-    wgu = gather(jnp.concatenate([columns(w_gate), columns(w_up)], 1)).reshape(tensor, model, -1)
-    wd = gather(lines(w_down)).reshape(tensor, -1, model)
+    deep = model // pairs
+    rest = gather(jnp.concatenate(
+        [columns(w_gate), columns(w_up), lines(w_down).reshape(deep, -1),
+         lines(w_output).reshape(deep, -1)], 1))
+    two = 2 * (w_gate.shape[1] // split)
+    wgu = rest[:, :two].reshape(tensor, model, two)
+    wd = rest[:, two : two + two // 2].reshape(tensor, two // 2, model)
+    wo = rest[:, two + two // 2 :].reshape(tensor, qw, model)
 
     gain_one = first_gain.astype(F32)
     gain_two = second_gain.astype(F32)
@@ -406,25 +411,22 @@
     back_one, share_one = norm_backward(dh_own, unit_one, inv_one, gain_one)
     input_grad = (mid_grad + back_one).astype(BF)
 
-    def reduce(w):
-        return lax.psum_scatter(w.reshape(-1, w.shape[-1]), spread, scatter_dimension=0, tiled=True)
-
-    def from_columns(w):
-        deep, cols = w.shape
-        w = lax.all_gather(w, home, axis=0, tiled=True).reshape(pairs, split, deep, cols)
-        return w
+    def total(wide, lined):
+        cols = wide.shape[-1]
+        packed = jnp.concatenate(
+            [wide.reshape(-1, cols), lined.reshape(tensor * model, -1)], axis=1)
+        packed = lax.psum_scatter(packed, spread, scatter_dimension=0, tiled=True)
+        packed = lax.all_gather(packed, home, axis=0, tiled=True)
+        packed = packed.reshape(pairs, split, deep, -1)
+        lined = packed[..., cols:].transpose(1, 0, 2, 3).reshape(-1, model)
+        return packed[..., :cols], lined.astype(F32)
 
     def join(w, start, cols):
         w = w[..., start : start + cols]
         return w.transpose(0, 2, 1, 3).reshape(model, split * cols).astype(F32)
 
-    def from_lines(w):
-        return lax.all_gather(w, ("core", "pair"), axis=0, tiled=True).astype(F32)
-
-    gu = from_columns(reduce(dgu))
-    down_wgrad = from_lines(reduce(dwd))
-    out_wgrad = from_lines(reduce(dwo))
-    qkv = from_columns(reduce(jnp.stack(terms)))
+    gu, down_wgrad = total(dgu, dwd)
+    qkv, out_wgrad = total(jnp.stack(terms), dwo)
     fw = gu.shape[-1] // 2
     kw = (qkv.shape[-1] - qw) // 2
     shares = jnp.sum(shares, axis=(0, 1))

time: 1020 us -> 1040 us (1.020)
  local copies, waits for them, and re-layouts: 57.8 us -> 93.8 us
  waiting for transfers between devices: 497 us -> 478 us
  other arithmetic: 69 us -> 84.2 us
    all_gather x4 -> x2, waiting for transfers between devices: 140 us -> 72.3 us  [gather(): return lax.all_gather(w, spread, axis=0, tiled=True)]
    reduce_scatter x4 -> x2, waiting for transfers between devices: 260 us -> 307 us  [total(): packed = lax.psum_scatter(packed, spread, scatter_dimension=0, tiled=True)]
    reshape x0 -> x6, local copies, waits for them, and re-layouts: none -> 18.5 us  [the longest x2 8.77 us: total(): lined.reshape(tensor * model, -1)]
    concatenate x1 -> x3, other arithmetic: 0.78 us -> 14.9 us  [the longest x2 13 us: total(): jnp.concatenate([wide.reshape(-1, cols), lined.reshape(tensor * model, -1...]
    slice x0 -> x3, local copies, waits for them, and re-layouts: none -> 11.5 us  [the longest x1 5.87 us: on_device(): wgu = rest[:, :two].reshape(tensor, model, two)]
  transfers between devices with their start and end apart: 24 -> 18, of which waited for: 15 -> 9; matrix products, arithmetic and copies ran while one was open for 19% -> 16% of each run, Pallas kernels for 16% -> 7%
where the time goes in v2:
time: 1040 us; the launch traced here: 1030 us
  waiting for transfers between devices  478 us (46%)
  Pallas kernels  230 us (22%)
  local copies, waits for them, and re-layouts  93.8 us (9%)
  other arithmetic  84.2 us (8%)
  matrix products  82.1 us (8%)
  blocking collectives  39.4 us (4%)
  between operations  15.2 us (1%)
    reduce_scatter x2, waiting for transfers between devices, total(): packed = lax.psum_scatter(packed, spread, scatter_dimension=0, tiled=True)  307 us
    pallas_call x1, Pallas kernels, attend_back(): pl.pallas_call(functools.partial(attend_back_kernel, halo, block, qw), gr...  94.7 us
    all_gather x2, waiting for transfers between devices, gather(): return lax.all_gather(w, spread, axis=0, tiled=True)  72.3 us
    pallas_call x1, Pallas kernels, attend(): pl.pallas_call(functools.partial(attend_kernel, halo, block, qw), grid=(s...  70.7 us
    pallas_call x1, Pallas kernels, feed(): pl.pallas_call(functools.partial(feed_kernel, rows // max(1, rows // 512)...  64.9 us
    dot_general x8, matrix products, nt(): lax.dot_general(left, right, (((1,), (1,)), ((), ())), preferred_element_...  58 us
    ppermute x1, waiting for transfers between devices, on_device(): lax.ppermute(tokens, 'tensor', [(d, d + h) for d in range(tensor - h)])  52.5 us
    psum x1, blocking collectives, on_device(): gains = lax.psum(gains, ('pair', 'core', 'tensor'))  39.4 us
  transfers between devices with their start and end apart: 18, of which 9 were waited for; matrix products, arithmetic and copies ran while one was open for 16% of the time, Pallas kernels for 7%

profile of v2, /device:TPU:0, one launch (start us, length us, event | category | flops | bytes accessed | tf_op | source)
XLA Modules:
  0.0 1031.7 jit_solution(13525046249882660787)
XLA Ops:
  16.7 5.0 collective-permute-start
  21.7 52.5 %collective-permute-done = bf16[768,1024]{1,0:T(8,128)(2,1)S(1)} collective-permute-done((bf16[768,1024]{1,0:T(8,128)(2,1)S(1)}, bf16[768,1024]{1,0:T(8,128)(2,1)S(1)}, u32[]{:S(2)}, u32[]{:S(2)}) %collective-permute-start) | collective-permute-done | bytes 1572896 | tf_op jit(solution)/shard_map/ppermute | solution.py:342
  77.5 4.6 collective-permute-done.2
  82.1 5.7 fusion.33
  88.7 5.2 fusion
  93.9 7.0 fusion.2.h_ref
  101.0 70.7 %shard_map.237 = (bf16[2,768,1024]{2,1,0:T(8,128)(2,1)}, f32[2,768,1024]{2,1,0:T(8,128)}) custom-call(s32[1]{0:T(128)} %bitcast.t_ref, bf16[2,1536,1024]{2,1,0:T(8,128)(2,1)} %fusion.2.h_ref, bf16[4,1024,512]{2,1,0:T(8,128)(2,1)} %bitcast.208, f32[2,1536,128]{2,1,0:T(8,128)S(1)} %get-tuple-element.65.cos_ref, f32[2,1536,128]{2,1,0:T(8,128)S(1)} %get-tuple-element.66.sin_ref, ...), custom_call_target="tpu_custom_call" | custom-call | flops 60000002048 | bytes 30000000 | tf_op jit(solution)/shard_map/pallas_call | solution.py:191
  171.7 72.3 %all-gather.7.cloned.1.call-done = bf16[4096,1408]{1,0:T(8,128)(2,1)} async-done(((bf16[256,1408]{1,0:T(8,128)(2,1)}), bf16[4096,1408]{1,0:T(8,128)(2,1)}) %all-gather.7.cloned.1.call-update) | async-done | bytes 11534352 | tf_op jit(solution)/shard_map/all_gather | solution.py:339
  248.6 6.0 fusion.40
  267.3 6.8 reshape.461.wd_ref
  274.2 5.9 slice.184
  283.8 4.6 copy.41
  288.4 64.9 %shard_map.238 = (f32[1536,1024]{1,0:T(8,128)}, f32[1536,1024]{1,0:T(8,128)}, bf16[4,1024,768]{2,1,0:T(8,128)(2,1)}, bf16[4,384,1024]{2,1,0:T(8,128)(2,1)}) custom-call(bf16[1536,1024]{1,0:T(8,128)(2,1)} %bitcast.184, bf16[1024,1536]{1,0:T(8,128)(2,1)} %bitcast.231, bf16[1536,1024]{1,0:T(8,128)(2,1)} %bitcast.230, bf16[4,1024,768]{2,1,0:T(8,128)(2,1)} %bitcast.198, ...), custom_call_target="tpu_custom_call" | custom-call | flops 49999998976 | bytes 40000000 | tf_op jit(solution)/shard_map/pallas_call | solution.py:284
  374.1 6.5 bitcast_convert_fusion
  380.7 94.7 %shard_map.239 = (bf16[4,2,768,256]{3,2,1,0:T(8,128)(2,1)}, bf16[4,2,1536,256]{3,2,1,0:T(8,128)(2,1)}, f32[4,2,8,128]{3,2,1,0:T(8,128)}) custom-call(s32[1]{0:T(128)} %bitcast.t_ref, bf16[2,1536,1024]{2,1,0:T(8,128)(2,1)} %fusion.2.h_ref, bf16[4,1024,512]{2,1,0:T(8,128)(2,1)} %bitcast.209, f32[2,1536,128]{2,1,0:T(8,128)} %copy-done.2, ...), custom_call_target="tpu_custom_call" | custom-call | flops 120000004096 | bytes 40000000 | tf_op jit(solution)/shard_map/pallas_call | solution.py:217
  492.5 5.3 maximum_maximum_fusion
  497.9 6.2 copy.42
  507.2 5.3 pad_maximum_fusion.2
  512.6 5.7 reshape.470
  518.3 7.7 pad_maximum_fusion
  526.0 154.3 %reduce-scatter.3.cloned.1.call-done = bf16[256,768]{1,0:T(8,128)(2,1)} async-done(((bf16[4096,768]{1,0:T(8,128)(2,1)}), bf16[256,768]{1,0:T(8,128)(2,1)}) %reduce-scatter.3.cloned.1.call-update) | async-done | bytes 393232 | tf_op jit(solution)/shard_map/reduce_scatter | solution.py:418
  680.4 7.6 fusion.31
  688.0 7.6 fusion.32
  695.6 7.6 fusion.30
  703.2 152.9 %reduce-scatter.5.cloned.1.call-done = bf16[256,1152]{1,0:T(8,128)(2,1)} async-done(((bf16[4096,1152]{1,0:T(8,128)(2,1)}), bf16[256,1152]{1,0:T(8,128)(2,1)}) %reduce-scatter.5.cloned.1.call-update) | async-done | bytes 589840 | tf_op jit(solution)/shard_map/reduce_scatter | solution.py:418
  856.1 18.8 %add_add_fusion = f32[3072,1024]{1,0:T(8,128)} fusion(f32[3072,1024]{1,0:T(8,128)} %fusion.30, f32[3072,1024]{1,0:T(8,128)} %fusion.32, f32[3072,1024]{1,0:T(8,128)} %fusion.31, bf16[3072,256]{1,0:T(8,128)(2,1)S(1)} %bitcast.195, bf16[4,1024,512]{2,1,0:T(8,128)(2,1)} %bitcast.213), kind=kOutput, calls=%fused_computation.5 | convolution fusion | flops 1620049920 | bytes 52428800 | tf_op jit(solution)/shard_map/dot_general | solution.py:37
  882.6 4.8 fusion.29
  887.4 7.3 add_add_fusion.1
  906.5 37.5 %collective-permute-done.11 = bf16[768,1024]{1,0:T(8,128)(2,1)} collective-permute-done((bf16[768,1024]{1,0:T(8,128)(2,1)}, bf16[768,1024]{1,0:T(8,128)(2,1)}, u32[]{:S(2)}, u32[]{:S(2)}) %collective-permute-start.11) | collective-permute-done | bytes 1572896 | tf_op jit(solution)/shard_map/ppermute | solution.py:408
  944.0 4.6 fusion.11
  948.6 39.4 %psum.7 = f32[2304]{0:T(1024)S(1)} all-reduce(f32[2304]{0:T(1024)S(1)} %pad_maximum_fusion.11), channel_id=1, replica_groups=mesh['pair'=4,'core'=2,'tensor'=4] {'pair','core','tensor'}, use_global_device_ids=true, to_apply=%region_8.0 | all-reduce | flops 2304 | bytes 18432 | tf_op jit(solution)/shard_map/psum | solution.py:435
  989.2 5.3 fusion.10
  (228 shorter events, 126.0 us)
Async XLA Ops:
  7.2 93.8 %all-gather.5.cloned.1.call-start = ((), (), s32[]{:S(2)}) async-start(), calls=%async_computation.2 | async-start | bytes 4456448 | tf_op jit(solution)/shard_map/all_gather | solution.py:339
  10.8 233.2 %all-gather.7.cloned.1.call-start = ((), (), s32[]{:S(2)}) async-start(), calls=%async_computation.3 | async-start | bytes 12255232 | tf_op jit(solution)/shard_map/all_gather | solution.py:339
  16.6 60.2 %copy-start.38 = (s32[3072]{0:T(1024)S(1)}, s32[3072]{0:T(1024)}, u32[]{:S(2)}) copy-start(s32[3072]{0:T(1024)} %param.15) | copy-start | bytes 36868
  16.6 60.8 %copy-start.41 = (bf16[128]{0:T(256)(128)(2,1)S(1)}, bf16[128]{0:T(256)(128)(2,1)}, u32[]{:S(2)}) copy-start(bf16[128]{0:T(256)(128)(2,1)} %param.21) | copy-start | bytes 772
  16.6 60.7 %copy-start.42 = (bf16[128]{0:T(256)(128)(2,1)S(1)}, bf16[128]{0:T(256)(128)(2,1)}, u32[]{:S(2)}) copy-start(bf16[128]{0:T(256)(128)(2,1)} %param.20) | copy-start | bytes 772
  16.6 60.8 %copy-start.39 = (bf16[1024]{0:T(1024)(128)(2,1)S(1)}, bf16[1024]{0:T(1024)(128)(2,1)}, u32[]{:S(2)}) copy-start(bf16[1024]{0:T(1024)(128)(2,1)} %param.16) | copy-start | bytes 6148
  16.6 663.7 %reduce-scatter.3.cloned.1.call-start = ((), (), s32[]{:S(2)}) async-start(), calls=%async_computation.4 | async-start | bytes 6684672 | tf_op jit(solution)/shard_map/reduce_scatter | solution.py:418
  16.7 57.5 %collective-permute-start = (bf16[768,1024]{1,0:T(8,128)(2,1)S(1)}, bf16[768,1024]{1,0:T(8,128)(2,1)S(1)}, u32[]{:S(2)}, u32[]{:S(2)}) collective-permute-start(bf16[768,1024]{1,0:T(8,128)(2,1)S(1)} %copy-done.7), channel_id=1, source_target_pairs={{0,1},{1,2},{2,3},{4,5},{5,6},{6,7},{8,9},{9,10},{10,11},{12,13},{... | collective-permute-start | bytes 4718600 | tf_op jit(solution)/shard_map/ppermute | solution.py:342
  76.8 11.9 %collective-permute-start.1 = (bf16[1536,1024]{1,0:T(8,128)(2,1)}, bf16[1536,1024]{1,0:T(8,128)(2,1)}, u32[]{:S(2)}, u32[]{:S(2)}) collective-permute-start(bf16[1536,1024]{1,0:T(8,128)(2,1)} %constant_dynamic-update-slice_fusion), channel_id=1, source_target_pairs={{0,4},{4,0},{1,5},{5,1},{2,6},{6,2},{3,7},{7,3},{8,12},{12,8},{9,1... | collective-permute-start | bytes 9437192 | tf_op jit(solution)/shard_map/ppermute | solution.py:322
  76.9 5.2 collective-permute-start.2
  77.4 23.6 %copy-start.4 = (f32[1,128]{1,0:T(1,128)}, f32[1,128]{1,0:T(1,128)S(1)}, u32[]{:S(2)}) copy-start(f32[1,128]{1,0:T(1,128)S(1)} %get-tuple-element.67.gk_ref) | copy-start | bytes 1540
  77.4 23.6 %copy-start.5 = (f32[1,128]{1,0:T(1,128)}, f32[1,128]{1,0:T(1,128)S(1)}, u32[]{:S(2)}) copy-start(f32[1,128]{1,0:T(1,128)S(1)} %get-tuple-element.68.gq_ref) | copy-start | bytes 1540
  77.4 16.5 %copy-start.33 = (f32[1024]{0:T(1024)}, f32[1024]{0:T(1024)S(1)}, u32[]{:S(2)}) copy-start(f32[1024]{0:T(1024)S(1)} %convert_element_type.189) | copy-start | bytes 12292
  88.6 12.4 %copy-start.2 = (f32[2,1536,128]{2,1,0:T(8,128)}, f32[2,1536,128]{2,1,0:T(8,128)S(1)}, u32[]{:S(2)}) copy-start(f32[2,1536,128]{2,1,0:T(8,128)S(1)} %get-tuple-element.65.cos_ref) | copy-start | bytes 4718596
  88.6 12.4 %copy-start.3 = (f32[2,1536,128]{2,1,0:T(8,128)}, f32[2,1536,128]{2,1,0:T(8,128)S(1)}, u32[]{:S(2)}) copy-start(f32[2,1536,128]{2,1,0:T(8,128)S(1)} %get-tuple-element.66.sin_ref) | copy-start | bytes 4718596
  254.9 3.5 collective-permute-start.3
  256.1 5.4 collective-permute-start.5
  261.3 19.0 %collective-permute-start.4 = (bf16[768,1024]{1,0:T(8,128)(2,1)}, bf16[768,1024]{1,0:T(8,128)(2,1)}, u32[]{:S(2)}, u32[]{:S(2)}) collective-permute-start(bf16[768,1024]{1,0:T(8,128)(2,1)} %multiply_convert_fusion), channel_id=1, source_target_pairs={{0,4},{4,0},{1,5},{5,1},{2,6},{6,2},{3,7},{7,3},{8,12},{12,8},{9,1... | collective-permute-start | bytes 4718600 | tf_op jit(solution)/shard_map/ppermute | solution.py:322
  355.5 3.5 collective-permute-start.7
  358.2 3.5 collective-permute-start.6
  365.2 5.0 collective-permute-start.8
  512.5 343.5 %reduce-scatter.5.cloned.1.call-start = ((), (), s32[]{:S(2)}) async-start(), calls=%async_computation.6 | async-start | bytes 10027008 | tf_op jit(solution)/shard_map/reduce_scatter | solution.py:418
  526.0 154.4 %copy-start.18 = (bf16[1,2,1536,256]{3,2,1,0:T(8,128)(2,1)S(1)}, bf16[1,2,1536,256]{3,2,1,0:T(8,128)(2,1)}, u32[]{:S(2)}) copy-start(bf16[1,2,1536,256]{3,2,1,0:T(8,128)(2,1)} %copy-done.17) | copy-start | bytes 4718596
  526.0 468.6 %all-gather.9.cloned.1.call-start = ((), (), s32[]{:S(2)}) async-start(), calls=%async_computation.5 | async-start | bytes 3538944 | tf_op jit(solution)/shard_map/all_gather | solution.py:419
  680.4 326.2 %all-gather.11.cloned.1.call-start = ((), (), s32[]{:S(2)}) async-start(), calls=%async_computation.7 | async-start | bytes 5308416 | tf_op jit(solution)/shard_map/all_gather | solution.py:419
  695.6 160.5 %copy-start.20 = (bf16[1,2,1536,256]{3,2,1,0:T(8,128)(2,1)S(1)}, bf16[1,2,1536,256]{3,2,1,0:T(8,128)(2,1)}, u32[]{:S(2)}) copy-start(bf16[1,2,1536,256]{3,2,1,0:T(8,128)(2,1)} %copy-done.19) | copy-start | bytes 4718596
  878.3 22.7 %collective-permute-start.10 = (bf16[768,1024]{1,0:T(8,128)(2,1)}, bf16[768,1024]{1,0:T(8,128)(2,1)}, u32[]{:S(2)}, u32[]{:S(2)}) collective-permute-start(bf16[768,1024]{1,0:T(8,128)(2,1)} %fusion.18), channel_id=1, source_target_pairs={{0,4},{4,0},{1,5},{5,1},{2,6},{6,2},{3,7},{7,3},{8,12},{12,8},{9,1... | collective-permute-start | bytes 4718600 | tf_op jit(solution)/shard_map/ppermute | solution.py:322
  900.6 43.3 %copy-start.34 = (f32[1024]{0:T(1024)S(1)}, f32[1024]{0:T(1024)}, u32[]{:S(2)}) copy-start(f32[1024]{0:T(1024)} %copy-done.33) | copy-start | bytes 12292
  900.6 5.8 collective-permute-start.9
  905.1 38.9 %collective-permute-start.11 = (bf16[768,1024]{1,0:T(8,128)(2,1)}, bf16[768,1024]{1,0:T(8,128)(2,1)}, u32[]{:S(2)}, u32[]{:S(2)}) collective-permute-start(bf16[768,1024]{1,0:T(8,128)(2,1)} %fusion.14), channel_id=1, source_target_pairs={{1,0},{2,1},{3,2},{5,4},{6,5},{7,6},{9,8},{10,9},{11,10},{13,12},{... | collective-permute-start | bytes 4718600 | tf_op jit(solution)/shard_map/ppermute | solution.py:408
  906.4 42.1 %copy-start.37 = (f32[1024]{0:T(1024)S(1)}, f32[1024]{0:T(1024)}, u32[]{:S(2)}) copy-start(f32[1024]{0:T(1024)} %get-tuple-element.33) | copy-start | bytes 12292
  906.4 82.8 %copy-start.9 = (bf16[768,1024]{1,0:T(8,128)(2,1)S(1)}, bf16[768,1024]{1,0:T(8,128)(2,1)}, u32[]{:S(2)}) copy-start(bf16[768,1024]{1,0:T(8,128)(2,1)} %param.14) | copy-start | bytes 4718596
  (39 other events, 191.7 us)
Sparse Core Ops, SparseCore 0:
  11.4 87.9 all-gather.4
  102.7 141.2 all-gather.6
  512.7 167.6 reduce-scatter.2
  685.9 170.1 reduce-scatter.4
  857.9 31.1 all-gather.8
  891.1 38.9 all-gather.10
